TPU v7x, 512 devices: a whole 4x8x8 slice. The times are simulated.
512 devices in a mesh: queue: 64 (over y, x, core), head: 8 (over z).
Axes of the slice: x: 4, y: 8, z: 8, core: 2. Of those that a mesh axis runs over, the one named last changes fastest.
Arguments:
- states: bfloat16 [16384, 3072], P('queue', 'head'), may hold values from -6 to 6
- noise: bfloat16 [512, 3072], P(None, 'head'), may hold values from -6 to 6
- w_qkv: bfloat16 [3072, 3, 3072], P('queue', None, 'head'), may hold values from -0.109375 to 0.109375
- w_out: bfloat16 [3072, 3072], P('head'), may hold values from -0.109375 to 0.109375
- w_mod: bfloat16 [256, 3, 3072], P(None, None, 'head'), may hold values from -0.375 to 0.375
- sigma_table: float32 [1000], replicated, may hold values from 0 to 1
- timesteps: int32 [64], replicated, may hold values from 0 to 999, as said below
- frame_index: int32 [64], replicated, may hold values from 0 to 127, as said below
Outputs:
- new_states: bfloat16 [16384, 3072], P('queue', 'head')
- velocity: bfloat16 [16384, 3072], P('queue', 'head')
Inputs may be any that keep to these rules, and one draw needn't show every extreme that they name: `timesteps`: strictly rising along the slots; slot 0 has 0 and the last slot 999. `frame_index`: strictly rising along the slots, by 1 to 3 from slot to slot; slot 0 holds 0 and the last slot 127.
All inputs are finite; a program needn't handle non-finite values.
Results may differ from a plain program's by a relative error of at most 0.023.
Values may be sent and summed in bfloat16 or wider, within the bound.
A program may use at most 64 MiB of HBM per device.

v0:
```python
import jax
import jax.numpy as jnp
from jax import lax
from jax.sharding import PartitionSpec as P

HD = 128
TEMB = 256
STEPS = 2


def from_behind(block, axis, distance):
    devices = range(lax.axis_size(axis))
    route = [(i - distance, i) for i in devices if i - distance in devices]
    return lax.ppermute(block, axis, route)


def frame_features(frame, first, count, width):
    half = width // 2
    feats = first + jnp.arange(count)
    index = jnp.where(feats < half, feats, feats - half).astype(jnp.float32)
    freq = jnp.exp(-jnp.log(10000.0) * index / half)
    angle = frame * freq
    return jnp.where(feats < half, jnp.sin(angle), jnp.cos(angle))


def time_features(value, count):
    half = count // 2
    freq = jnp.exp(-jnp.log(10000.0) * jnp.arange(half).astype(jnp.float32) / half)
    angle = value * freq
    return jnp.concatenate([jnp.cos(angle), jnp.sin(angle)])


def shards(states, noise, w_qkv, w_out, w_mod, sigma_table, timesteps, frame_index):
    queue_len = lax.axis_size("queue")
    device = lax.axis_index("queue")
    group = lax.axis_index("head")
    tokf = states.shape[0]
    local_width = states.shape[1]
    width = local_width * lax.axis_size("head")
    local_hh = w_out.shape[0]
    local_heads = local_hh // HD
    hidden = states
    velocity = None
    weight_buffer = None
    last = frame_index[queue_len - 1]
    for step in range(STEPS):
        ahead = device + step
        frame = jnp.where(
            ahead < queue_len,
            frame_index[jnp.minimum(ahead, queue_len - 1)],
            last + ahead - queue_len + 1,
        )
        frame = frame.astype(jnp.float32)
        tstep = timesteps[device]
        emb = time_features(tstep.astype(jnp.float32), TEMB)
        modul = jnp.dot(
            emb[None, :],
            w_mod.astype(jnp.float32).reshape(TEMB, 3 * local_width),
            precision=lax.Precision.HIGHEST,
        )
        modul = modul.reshape(3, local_width)
        u = (
            hidden.astype(jnp.float32)
            + frame_features(frame, group * local_width, local_width, width)[None, :]
        )
        sums, squares = lax.psum((jnp.sum(u, axis=1), jnp.sum(u * u, axis=1)), "head")
        mean = (sums / width)[:, None]
        var = (squares / width)[:, None] - mean * mean
        normed = (u - mean) / jnp.sqrt(var + 1e-06)
        local_mod = (normed * (1.0 + modul[1][None, :]) + modul[0][None, :]).astype(jnp.bfloat16)
        modded = lax.all_gather(local_mod, "head", axis=1, tiled=True)
        gate = modul[2]
        columns = 3 * local_hh
        if step == 0:
            piece = lax.all_gather(w_qkv, "queue", axis=0, tiled=True)
            rows = piece.shape[0]
            total = jnp.dot(
                modded, piece.reshape(rows, columns), preferred_element_type=jnp.float32
            )
            qkv = total
            weight_buffer = piece
        else:
            qkv = jnp.dot(
                modded, weight_buffer.reshape(width, columns), preferred_element_type=jnp.float32
            )
        qkv = qkv.astype(jnp.bfloat16).reshape(tokf, 3, local_hh)
        query = qkv[:, 0].reshape(tokf, local_heads, HD)
        own_kv = jnp.stack([qkv[:, 1], qkv[:, 2]])
        prev_kv = from_behind(own_kv, "queue", 1)
        all_keys = jnp.concatenate([own_kv[0], prev_kv[0]], axis=0).reshape(
            2 * tokf, local_heads, HD
        )
        all_values = jnp.concatenate([own_kv[1], prev_kv[1]], axis=0).reshape(
            2 * tokf, local_heads, HD
        )
        scores = jnp.einsum(
            "thd,shd->hts", query, all_keys, preferred_element_type=jnp.float32
        ) / jnp.sqrt(jnp.float32(HD))
        valid = (jnp.arange(2 * tokf) < tokf) | (device > 0)
        scores = jnp.where(valid[None, None, :], scores, -1e30)
        expo = jnp.exp(scores)
        probs = (expo / jnp.sum(expo, axis=2, keepdims=True)).astype(jnp.bfloat16)
        attn = jnp.einsum("hts,shd->thd", probs, all_values, preferred_element_type=jnp.float32)
        attn = attn.astype(jnp.bfloat16).reshape(tokf, local_hh)
        terms = jnp.dot(attn, w_out, preferred_element_type=jnp.float32)
        summed = lax.psum_scatter(
            terms.astype(jnp.bfloat16), "head", scatter_dimension=1, tiled=True
        ).astype(jnp.float32)
        vel = gate[None, :] * summed
        velocity = vel.astype(jnp.bfloat16)
        sig_now = sigma_table[tstep]
        sig_target = jnp.where(device > 0, sigma_table[timesteps[jnp.maximum(device - 1, 0)]], 0.0)
        updated = (hidden.astype(jnp.float32) + (sig_target - sig_now) * vel).astype(jnp.bfloat16)
        fresh = noise[step * tokf : (step + 1) * tokf]
        moved = from_behind(updated, "queue", -1)
        hidden = jnp.where(device == queue_len - 1, fresh, moved)
    return (hidden, velocity)


def solution(mesh):
    in_specs = (
        P("queue", "head"),
        P(None, "head"),
        P("queue", None, "head"),
        P("head", None),
        P(None, None, "head"),
        P(),
        P(),
        P(),
    )
    out_specs = (P("queue", "head"), P("queue", "head"))
    return jax.shard_map(shards, mesh=mesh, in_specs=in_specs, out_specs=out_specs, check_vma=False)
```

profile of v0, /device:TPU:31, one launch (start us, length us, event | category | flops | bytes accessed | tf_op | source)
XLA Modules:
  0.0 374.2 jit_solution(12738407828771928669)
XLA Ops:
  7.2 0.0 all-gather.6.cloned.1.call-start
  7.2 0.7 all-gather.6.cloned.1.call-update
  7.9 0.0 all-gather.4.cloned.1.call-start
  8.0 1.3 fusion.52
  9.9 1.4 fusion.53
  12.6 1.3 copy.30
  13.9 0.1 cosine_select_fusion.1
  14.0 1.1 fusion.7
  15.1 19.4 %all-reduce.1 = (f32[256]{0:T(256)S(1)}, f32[256]{0:T(256)S(1)}) all-reduce(f32[256]{0:T(256)S(1)} %get-tuple-element.5, f32[256]{0:T(256)S(1)} %get-tuple-element.4), channel_id=1, replica_groups=mesh['queue'=64,'head'=8] {'head'}, use_global_device_ids=true, to_apply=%region_3.4 | all-reduce | flops 512 | bytes 4096 | tf_op jit(solution)/shard_map/psum | solution.py:66
  34.6 0.6 convolution_reduce_fusion
  35.2 0.8 fusion.11
  36.1 0.0 all-gather.4.cloned.1.call-update
  36.1 0.0 reduce-scatter.7.cloned.1.call-start
  36.1 64.5 %all-gather.6.cloned.1.call-done = bf16[3072,3,384]{2,0,1:T(8,128)(2,1)} async-done(((bf16[48,3,384]{2,0,1:T(8,128)(2,1)}), bf16[3072,3,384]{2,0,1:T(8,128)(2,1)}) %all-gather.6.cloned.1.call-update) | async-done | bytes 7077904 | tf_op jit(solution)/shard_map/all_gather | solution.py:75
  100.7 10.3 %copy.31 = bf16[3072,3,384]{0,2,1:T(8,128)(2,1)} copy(bf16[3072,3,384]{2,0,1:T(8,128)(2,1)} %all-gather.6.cloned.1.call-done) | data formatting | bytes 14155776 | tf_op jit(solution)/shard_map/all_gather | solution.py:75
  111.0 30.9 %all-gather.4.cloned.1.call-done = bf16[256,3072]{1,0:T(8,128)(2,1)} async-done(((bf16[256,384]{1,0:T(8,128)(2,1)}), bf16[256,3072]{1,0:T(8,128)(2,1)}) %all-gather.4.cloned.1.call-update) | async-done | bytes 1572880 | tf_op jit(solution)/shard_map/all_gather | solution.py:71
  141.9 6.6 %convolution_convert_fusion.3 = bf16[256,1152]{1,0:T(8,128)(2,1)} fusion(bf16[256,3072]{1,0:T(8,128)(2,1)} %all-gather.4.cloned.1.call-done, bf16[3072,1152]{0,1:T(8,128)(2,1)} %bitcast.54), kind=kOutput, calls=%fused_computation.3 | convolution fusion | flops 1812234240 | bytes 9240576 | tf_op jit(solution)/shard_map/dot_general | solution.py:77
  148.4 1.3 copy.32
  149.7 0.7 fusion.47
  150.5 0.8 pad_maximum_fusion
  151.2 9.0 %collective-permute-start = (bf16[2,256,384]{1,2,0:T(8,128)(2,1)}, bf16[2,256,384]{1,2,0:T(8,128)(2,1)S(1)}, u32[]{:S(2)}, u32[]{:S(2)}) collective-permute-start(bf16[2,256,384]{1,2,0:T(8,128)(2,1)} %pad_maximum_fusion), channel_id=1, source_target_pairs={{0,8},{8,16},{16,24},{24,32},{32,40},{40,48},{48,56},{56,64},{64,7... | collective-permute-start | bytes 1179656 | tf_op jit(solution)/shard_map/ppermute | solution.py:14
  160.3 0.8 copy.35
  161.1 4.2 %collective-permute-done = bf16[2,256,384]{1,2,0:T(8,128)(2,1)S(1)} collective-permute-done((bf16[2,256,384]{1,2,0:T(8,128)(2,1)}, bf16[2,256,384]{1,2,0:T(8,128)(2,1)S(1)}, u32[]{:S(2)}, u32[]{:S(2)}) %collective-permute-start) | collective-permute-done | bytes 393248 | tf_op jit(solution)/shard_map/ppermute | solution.py:14
  165.3 0.7 fusion.49
  166.0 0.2 copy.36
  166.1 2.7 select_exponential_fusion.1
  168.9 2.4 convolution_convert_fusion.5
  171.3 2.2 convolution_convert_fusion.1
  173.5 2.7 copy.48
  176.2 0.0 reduce-scatter.7.cloned.1.call-update
  176.2 0.0 all-gather.8.cloned.1.call-start
  179.8 1.4 fusion.51
  182.5 32.3 %reduce-scatter.7.cloned.1.call-done = bf16[384,256]{1,0:T(8,128)(2,1)} async-done(((bf16[3072,256]{1,0:T(8,128)(2,1)}), bf16[384,256]{1,0:T(8,128)(2,1)}) %reduce-scatter.7.cloned.1.call-update) | async-done | bytes 196624
  214.8 1.1 copy.49
  215.8 0.1 fusion.13
  215.9 6.5 %collective-permute-start.1 = (bf16[256,384]{1,0:T(8,128)(2,1)S(1)}, bf16[256,384]{1,0:T(8,128)(2,1)S(1)}, u32[]{:S(2)}, u32[]{:S(2)}) collective-permute-start(bf16[256,384]{1,0:T(8,128)(2,1)S(1)} %fusion.13), channel_id=1, source_target_pairs={{8,0},{16,8},{24,16},{32,24},{40,32},{48,40},{56,48},{64,56},{72,6... | collective-permute-start | bytes 589832 | tf_op jit(solution)/shard_map/ppermute | solution.py:14
  223.8 0.1 cosine_select_fusion
  223.8 4.3 %collective-permute-done.1 = bf16[256,384]{1,0:T(8,128)(2,1)S(1)} collective-permute-done((bf16[256,384]{1,0:T(8,128)(2,1)S(1)}, bf16[256,384]{1,0:T(8,128)(2,1)S(1)}, u32[]{:S(2)}, u32[]{:S(2)}) %collective-permute-start.1) | collective-permute-done | bytes 196640 | tf_op jit(solution)/shard_map/ppermute | solution.py:14
  228.1 0.2 fusion.4
  228.3 11.7 %all-reduce = (f32[256]{0:T(256)S(1)}, f32[256]{0:T(256)S(1)}) all-reduce(f32[256]{0:T(256)S(1)} %get-tuple-element.3, f32[256]{0:T(256)S(1)} %get-tuple-element.2), channel_id=1, replica_groups=mesh['queue'=64,'head'=8] {'head'}, use_global_device_ids=true, to_apply=%region_9.10 | all-reduce | flops 512 | bytes 4096 | tf_op jit(solution)/shard_map/psum | solution.py:66
  240.1 0.8 fusion.17
  240.9 0.0 all-gather.8.cloned.1.call-update
  240.9 0.0 reduce-scatter.9.cloned.1.call-start
  241.0 39.3 %all-gather.8.cloned.1.call-done = bf16[256,3072]{1,0:T(8,128)(2,1)} async-done(((bf16[256,384]{1,0:T(8,128)(2,1)}), bf16[256,3072]{1,0:T(8,128)(2,1)}) %all-gather.8.cloned.1.call-update) | async-done | bytes 1572880 | tf_op jit(solution)/shard_map/all_gather | solution.py:71
  280.2 6.6 %convolution_convert_fusion.2 = bf16[256,1152]{1,0:T(8,128)(2,1)} fusion(bf16[256,3072]{1,0:T(8,128)(2,1)} %all-gather.8.cloned.1.call-done, bf16[3072,1152]{0,1:T(8,128)(2,1)} %bitcast.55), kind=kOutput, calls=%fused_computation.2 | convolution fusion | flops 1812234240 | bytes 9240576 | tf_op jit(solution)/shard_map/dot_general | solution.py:83
  286.9 1.3 copy.38
  288.2 0.7 fusion.46
  288.9 0.8 pad_maximum_fusion.1
  289.7 9.0 %collective-permute-start.2 = (bf16[2,256,384]{1,2,0:T(8,128)(2,1)}, bf16[2,256,384]{1,2,0:T(8,128)(2,1)S(1)}, u32[]{:S(2)}, u32[]{:S(2)}) collective-permute-start(bf16[2,256,384]{1,2,0:T(8,128)(2,1)} %pad_maximum_fusion.1), channel_id=1, source_target_pairs={{0,8},{8,16},{16,24},{24,32},{32,40},{40,48},{48,56},{56,64},{64,7... | collective-permute-start | bytes 1179656 | tf_op jit(solution)/shard_map/ppermute | solution.py:14
  298.7 0.8 copy.41
  299.5 4.2 %collective-permute-done.2 = bf16[2,256,384]{1,2,0:T(8,128)(2,1)S(1)} collective-permute-done((bf16[2,256,384]{1,2,0:T(8,128)(2,1)}, bf16[2,256,384]{1,2,0:T(8,128)(2,1)S(1)}, u32[]{:S(2)}, u32[]{:S(2)}) %collective-permute-start.2) | collective-permute-done | bytes 393248 | tf_op jit(solution)/shard_map/ppermute | solution.py:14
  303.7 0.7 fusion.48
  304.4 0.2 copy.42
  304.6 2.7 select_exponential_fusion
  307.2 2.4 convolution_convert_fusion.4
  309.6 2.2 convolution_convert_fusion
  311.8 2.6 copy.50
  314.4 0.0 reduce-scatter.9.cloned.1.call-update
  314.4 38.6 %reduce-scatter.9.cloned.1.call-done = bf16[384,256]{1,0:T(8,128)(2,1)} async-done(((bf16[3072,256]{1,0:T(8,128)(2,1)}), bf16[384,256]{1,0:T(8,128)(2,1)}) %reduce-scatter.9.cloned.1.call-update) | async-done | bytes 196624
  352.9 1.1 copy.51
  354.0 0.8 fusion.32
  354.8 6.6 %collective-permute-start.3 = (bf16[256,384]{1,0:T(8,128)(2,1)S(1)}, bf16[256,384]{1,0:T(8,128)(2,1)S(1)}, u32[]{:S(2)}, u32[]{:S(2)}) collective-permute-start(bf16[256,384]{1,0:T(8,128)(2,1)S(1)} %get-tuple-element.26), channel_id=1, source_target_pairs={{8,0},{16,8},{24,16},{32,24},{40,32},{48,40},{56,48},{64,56},{72,6... | collective-permute-start | bytes 589832 | tf_op jit(solution)/shard_map/ppermute | solution.py:14
  361.4 5.6 %collective-permute-done.3 = bf16[256,384]{1,0:T(8,128)(2,1)S(1)} collective-permute-done((bf16[256,384]{1,0:T(8,128)(2,1)S(1)}, bf16[256,384]{1,0:T(8,128)(2,1)S(1)}, u32[]{:S(2)}, u32[]{:S(2)}) %collective-permute-start.3) | collective-permute-done | bytes 196640 | tf_op jit(solution)/shard_map/ppermute | solution.py:14
  367.0 0.7 slice_select_fusion.1
  (18 shorter events, 0.1 us)
Async XLA Ops:
  7.2 164.1 %copy-start = (bf16[384,3072]{1,0:T(8,128)(2,1)S(1)}, bf16[384,3072]{1,0:T(8,128)(2,1)}, u32[]{:S(2)}) copy-start(bf16[384,3072]{1,0:T(8,128)(2,1)} %param.11) | copy-start | bytes 7077892
  7.2 28.0 %copy-start.1 = (bf16[256,384]{1,0:T(8,128)(2,1)S(1)}, bf16[256,384]{1,0:T(8,128)(2,1)}, u32[]{:S(2)}) copy-start(bf16[256,384]{1,0:T(8,128)(2,1)} %param.8) | copy-start | bytes 589828
  7.2 93.5 %all-gather.6.cloned.1.call-start = ((), (), s32[]{:S(2)}) async-start(), calls=%async_computation.3 | async-start | bytes 7188480 | tf_op jit(solution)/shard_map/all_gather | solution.py:75
  7.9 133.9 %all-gather.4.cloned.1.call-start = ((), (), s32[]{:S(2)}) async-start(), calls=%async_computation.2 | async-start | bytes 1769472 | tf_op jit(solution)/shard_map/all_gather | solution.py:71
  36.1 178.7 %reduce-scatter.7.cloned.1.call-start = ((), (), s32[]{:S(2)}) async-start(), calls=%async_computation.5 | async-start | bytes 1769472
  151.2 14.0 %collective-permute-start = (bf16[2,256,384]{1,2,0:T(8,128)(2,1)}, bf16[2,256,384]{1,2,0:T(8,128)(2,1)S(1)}, u32[]{:S(2)}, u32[]{:S(2)}) collective-permute-start(bf16[2,256,384]{1,2,0:T(8,128)(2,1)} %pad_maximum_fusion), channel_id=1, source_target_pairs={{0,8},{8,16},{16,24},{24,32},{32,40},{40,48},{48,56},{56,64},{64,7... | collective-permute-start | bytes 1179656 | tf_op jit(solution)/shard_map/ppermute | solution.py:14
  166.0 2.9 copy-start.5
  176.2 51.9 %copy-start.2 = (bf16[512,384]{1,0:T(8,128)(2,1)S(1)}, bf16[512,384]{1,0:T(8,128)(2,1)}, u32[]{:S(2)}) copy-start(bf16[512,384]{1,0:T(8,128)(2,1)} %param.9) | copy-start | bytes 1179652
  176.2 104.1 %all-gather.8.cloned.1.call-start = ((), (), s32[]{:S(2)}) async-start(), calls=%async_computation.4 | async-start | bytes 1769472 | tf_op jit(solution)/shard_map/all_gather | solution.py:71
  215.9 12.2 %collective-permute-start.1 = (bf16[256,384]{1,0:T(8,128)(2,1)S(1)}, bf16[256,384]{1,0:T(8,128)(2,1)S(1)}, u32[]{:S(2)}, u32[]{:S(2)}) collective-permute-start(bf16[256,384]{1,0:T(8,128)(2,1)S(1)} %fusion.13), channel_id=1, source_target_pairs={{8,0},{16,8},{24,16},{32,24},{40,32},{48,40},{56,48},{64,56},{72,6... | collective-permute-start | bytes 589832 | tf_op jit(solution)/shard_map/ppermute | solution.py:14
  240.9 112.0 %reduce-scatter.9.cloned.1.call-start = ((), (), s32[]{:S(2)}) async-start(), calls=%async_computation.6 | async-start | bytes 1769472
  289.7 14.0 %collective-permute-start.2 = (bf16[2,256,384]{1,2,0:T(8,128)(2,1)}, bf16[2,256,384]{1,2,0:T(8,128)(2,1)S(1)}, u32[]{:S(2)}, u32[]{:S(2)}) collective-permute-start(bf16[2,256,384]{1,2,0:T(8,128)(2,1)} %pad_maximum_fusion.1), channel_id=1, source_target_pairs={{0,8},{8,16},{16,24},{24,32},{32,40},{40,48},{48,56},{56,64},{64,7... | collective-permute-start | bytes 1179656 | tf_op jit(solution)/shard_map/ppermute | solution.py:14
  304.4 2.8 copy-start.4
  314.4 52.6 %copy-start.3 = (bf16[512,384]{1,0:T(8,128)(2,1)S(1)}, bf16[512,384]{1,0:T(8,128)(2,1)}, u32[]{:S(2)}) copy-start(bf16[512,384]{1,0:T(8,128)(2,1)} %param.9) | copy-start | bytes 1179652
  354.8 12.1 %collective-permute-start.3 = (bf16[256,384]{1,0:T(8,128)(2,1)S(1)}, bf16[256,384]{1,0:T(8,128)(2,1)S(1)}, u32[]{:S(2)}, u32[]{:S(2)}) collective-permute-start(bf16[256,384]{1,0:T(8,128)(2,1)S(1)} %get-tuple-element.26), channel_id=1, source_target_pairs={{8,0},{16,8},{24,16},{32,24},{40,32},{48,40},{56,48},{64,56},{72,6... | collective-permute-start | bytes 589832 | tf_op jit(solution)/shard_map/ppermute | solution.py:14
Sparse Core Ops, SparseCore 0:
  11.3 89.2 all-gather.5
  103.3 38.4 all-gather.3
  176.3 38.4 reduce-scatter.6
  241.0 39.1 all-gather.7
  314.5 38.4 reduce-scatter.8
where the time goes:
time: 375 us; the launch traced here: 374 us
  waiting for transfers between devices  225 us (60%)
  starting transfers between devices  31.3 us (8%)
  blocking collectives  31.2 us (8%)
  local copies, waits for them, and re-layouts  30.6 us (8%)
  matrix products  28.3 us (8%)
  between operations  22.1 us (6%)
  other arithmetic  6.29 us (2%)
    unnamed x7, waiting for transfers between devices  71.6 us
    all_gather x2, waiting for transfers between devices, shards(): modded = lax.all_gather(local_mod, 'head', axis=1, tiled=True)  70.2 us
    all_gather x1, waiting for transfers between devices, shards(): piece = lax.all_gather(w_qkv, 'queue', axis=0, tiled=True)  64.5 us
    psum x2, blocking collectives, shards(): lax.psum((jnp.sum(u, axis=1), jnp.sum(u * u, axis=1)), 'head')  31.2 us
    ppermute x4, starting transfers between devices, from_behind(): return lax.ppermute(block, axis, route)  31.1 us
    ppermute x4, waiting for transfers between devices, from_behind(): return lax.ppermute(block, axis, route)  18.2 us
    all_gather x1, local copies, waits for them, and re-layouts, shards(): piece = lax.all_gather(w_qkv, 'queue', axis=0, tiled=True)  10.3 us
    unnamed x17, local copies, waits for them, and re-layouts  8.76 us
  transfers between devices with their start and end apart: 9, of which 9 were waited for; matrix products, arithmetic and copies ran while one was open for 5% of the time, Pallas kernels for 0%

commit v1 on v0

v1 whole, which is shorter than its diff:
```python
import functools
import math

import jax
import jax.numpy as jnp
import numpy as np
from jax import lax
from jax.experimental import pallas as pl
from jax.experimental.pallas import tpu as pltpu
from jax.sharding import PartitionSpec as P

MESH = pl.DeviceIdType.MESH
HD = 128
TEMB = 256
STEPS = 2
NX = 4
NY = 8
CORES = 2
LANES = 128
F32 = jnp.float32
BF16 = jnp.bfloat16


def frequencies(half):
    return np.exp(-np.log(10000.0) * np.arange(half) / half).astype(np.float32)


def kernel(
    queue_len,
    nz,
    sigma_ref,
    tsteps_ref,
    frames_ref,
    pfreq_ref,
    tfreq_ref,
    states_ref,
    wq_ref,
    wm_hbm,
    wo_hbm,
    noise_hbm,
    new_ref,
    vel_ref,
    xg,
    h,
    wg,
    wo,
    wm,
    acc,
    query,
    kv,
    prev,
    attn,
    rs_out,
    rs_in,
    upd,
    fresh,
    pos,
    sg,
    modg,
    mean_b,
    rstd_b,
    wo_sem,
    wm_sem,
    noise_sem,
    ag_send,
    ag_recv,
    w_send,
    w_recv,
    s_send,
    s_recv,
    st_send,
    st_recv,
    mod_send,
    mod_recv,
    kv_send,
    kv_recv,
    rs_send,
    rs_recv,
    sh_send,
    sh_recv,
):
    q = lax.axis_index("queue")
    z = lax.axis_index("head")
    core = lax.rem(q, CORES)
    x = lax.rem(q // CORES, NX)
    y = q // (CORES * NX)
    tokf, width = states_ref.shape
    half = tokf // 2
    full = width * nz
    tiles = width // LANES
    local_hh = wo.shape[1]
    heads = local_hh // HD

    def ring(base, offset, size):
        return lax.rem(base + offset + size, size)

    def queue_id(yy, xx, cc):
        return (yy * NX + xx) * CORES + cc

    def at_z(offset):
        return (q, ring(z, offset, nz))

    def at_x(offset):
        return (queue_id(y, ring(x, offset, NX), core), z)

    def at_y(offset):
        return (queue_id(ring(y, offset, NY), x, core), z)

    sibling = (queue_id(y, x, 1 - core), z)
    after = (ring(q, 1, queue_len), z)
    before = (ring(q, -1, queue_len), z)
    last_slot = q == queue_len - 1

    def remote(src, dst, send, recv, device):
        return pltpu.make_async_remote_copy(
            src_ref=src, dst_ref=dst, send_sem=send, recv_sem=recv, device_id=device, device_id_type=MESH
        )

    barrier = pltpu.get_barrier_semaphore()
    partners = [at_z(d) for d in range(1, nz)]
    partners += [at_x(1), at_x(-1), at_y(1), at_y(-1), sibling, after, before]
    for partner in partners:
        pl.semaphore_signal(barrier, inc=1, device_id=partner, device_id_type=MESH)

    wm_copy = pltpu.make_async_copy(wm_hbm, wm, wm_sem)
    wm_copy.start()
    wo_copies = [
        pltpu.make_async_copy(wo_hbm.at[:, b * width : (b + 1) * width], wo.at[b], wo_sem.at[b]) for b in range(nz)
    ]
    for copy in wo_copies:
        copy.start()
    noise_copy = pltpu.make_async_copy(noise_hbm, fresh, noise_sem)

    @pl.when(last_slot)
    def _():
        noise_copy.start()

    xg[0, z] = states_ref[...]
    for c in range(3):
        wg[y, x, core, :, c * local_hh : (c + 1) * local_hh] = wq_ref[c]

    tstep = tsteps_ref[q]
    sig_now = sigma_ref[tstep]
    sig_before = sigma_ref[tsteps_ref[jnp.maximum(q - 1, 0)]]
    sig_step = jnp.where(q > 0, sig_before, 0.0) - sig_now
    last_frame = frames_ref[queue_len - 1]

    block = lax.broadcasted_iota(jnp.int32, (nz, width), 0)
    for step in range(STEPS):
        ahead = q + step
        frame = jnp.where(
            ahead < queue_len, frames_ref[jnp.minimum(ahead, queue_len - 1)], last_frame + ahead - queue_len + 1
        )
        angle = frame.astype(F32) * pfreq_ref[...]
        pos[step] = jnp.where(block < nz // 2, jnp.sin(angle), jnp.cos(angle))

    def lanes(t):
        return slice(t * LANES, (t + 1) * LANES)

    def own_sums(step):
        row = pos[step, pl.ds(z, 1), :]
        sums = jnp.zeros((tokf, LANES), F32)
        squares = jnp.zeros((tokf, LANES), F32)
        for t in range(tiles):
            u = xg[step, z, :, lanes(t)].astype(F32) + row[:, lanes(t)]
            sums = sums + u
            squares = squares + u * u
        sums = jnp.sum(sums, axis=1, keepdims=True)
        squares = jnp.sum(squares, axis=1, keepdims=True)
        lane = lax.broadcasted_iota(jnp.int32, (tokf, LANES), 1)
        both = jnp.where(lane == 0, sums, jnp.where(lane == 1, squares, 0.0))
        sg[step, z] = both.T[0:8]

    def sums_copy(step, d):
        return remote(sg.at[step, z], sg.at[step, z], st_send.at[step, d], st_recv.at[step, d], at_z(d))

    def sums_arrival(step, d):
        k = ring(z, -d, nz)
        return remote(sg.at[step, k], sg.at[step, k], st_send.at[step, d], st_recv.at[step, d], at_z(d))

    def finish_sums(step):
        for d in range(1, nz):
            sums_arrival(step, d).wait_recv()
        total = sg[step, 0]
        for k in range(1, nz):
            total = total + sg[step, k]
        mean = total[0:1] / full
        var = total[1:2] / full - mean * mean
        rstd = lax.rsqrt(var + 1e-06)
        mean_b[...] = jnp.broadcast_to(mean, (LANES, tokf)).T
        rstd_b[...] = jnp.broadcast_to(rstd, (LANES, tokf)).T

    def ag_part(step, k, direction, r):
        if r < nz // 2 - 1:
            return xg.at[step, k]
        return xg.at[step, k, pl.ds(direction * half, half), :]

    def ag_copy(step, direction, r):
        k = ring(z, -r if direction == 0 else r, nz)
        ref = ag_part(step, k, direction, r)
        return remote(
            ref, ref, ag_send.at[step, direction, r], ag_recv.at[step, direction, r], at_z(1 if direction == 0 else -1)
        )

    def ag_arrival(step, direction, r):
        k = ring(z, -r - 1 if direction == 0 else r + 1, nz)
        ref = ag_part(step, k, direction, r)
        return remote(
            ref, ref, ag_send.at[step, direction, r], ag_recv.at[step, direction, r], at_z(1 if direction == 0 else -1)
        )

    def modulate(step, k):
        row = pos[step, pl.ds(k, 1), :]
        rows = modg[k]
        shift, scale = rows[0:1], 1.0 + rows[1:2]
        for t in range(tiles):
            u = xg[step, k, :, lanes(t)].astype(F32) + row[:, lanes(t)]
            normed = (u - mean_b[...]) * rstd_b[...]
            h[k, :, lanes(t)] = (normed * scale[:, lanes(t)] + shift[:, lanes(t)]).astype(BF16)

    def project(k):
        weights = wg[k].reshape(width, 3 * local_hh)
        acc[...] += jnp.dot(h[k], weights, preferred_element_type=F32)

    def w_copy(index, ref, device):
        return remote(ref, ref, w_send.at[index], w_recv.at[index], device)

    def s_copy(index, ref):
        return remote(ref, ref, s_send.at[index], s_recv.at[index], sibling)

    xr = [ring(x, k, NX) for k in range(NX)]
    yr = [ring(y, k, NY) for k in range(NY)]
    far = NY // 2

    c0_send = {
        0: (wg.at[y, x, 0], at_x(1)),
        1: (wg.at[y, x, 0], at_x(-1)),
        2: (wg.at[y, xr[3], 0], at_x(1)),
    }
    c0_recv = {0: wg.at[y, xr[3], 0], 1: wg.at[y, xr[1], 0], 2: wg.at[y, xr[2], 0]}
    for r in range(far):
        up, down = yr[-r % NY], yr[r]
        up_next, down_next = yr[(-r - 1) % NY], yr[r + 1]
        if r < far - 1:
            c0_send[3 + 2 * r] = (wg.at[up, :, 0], at_y(1))
            c0_send[4 + 2 * r] = (wg.at[down, :, 0], at_y(-1))
            c0_recv[3 + 2 * r] = wg.at[up_next, :, 0]
            c0_recv[4 + 2 * r] = wg.at[down_next, :, 0]
        else:
            c0_send[3 + 2 * r] = (wg.at[up, pl.ds(0, 2), 0], at_y(1))
            c0_send[4 + 2 * r] = (wg.at[down, pl.ds(2, 2), 0], at_y(-1))
            c0_recv[3 + 2 * r] = wg.at[up_next, pl.ds(0, 2), 0]
            c0_recv[4 + 2 * r] = wg.at[down_next, pl.ds(2, 2), 0]
    c1_send, c1_recv = {}, {}
    for r in range(far):
        up, down = yr[-r % NY], yr[r]
        up_next, down_next = yr[(-r - 1) % NY], yr[r + 1]
        if r < far - 1:
            c1_send[2 * r] = (wg.at[up, x, 1], at_y(1))
            c1_send[2 * r + 1] = (wg.at[down, x, 1], at_y(-1))
            c1_recv[2 * r] = wg.at[up_next, x, 1]
            c1_recv[2 * r + 1] = wg.at[down_next, x, 1]
        else:
            c1_send[2 * r] = (wg.at[up, x, 1, pl.ds(0, 32)], at_y(1))
            c1_send[2 * r + 1] = (wg.at[down, x, 1, pl.ds(32, 16)], at_y(-1))
            c1_recv[2 * r] = wg.at[up_next, x, 1, pl.ds(0, 32)]
            c1_recv[2 * r + 1] = wg.at[down_next, x, 1, pl.ds(32, 16)]
    c1_send[8] = (wg.at[:, x, 1], at_x(1))
    c1_send[9] = (wg.at[:, x, 1], at_x(-1))
    c1_recv[8] = wg.at[:, xr[3], 1]
    c1_recv[9] = wg.at[:, xr[1], 1]
    c1_send[10] = (wg.at[pl.ds(0, far), xr[3], 1], at_x(1))
    c1_send[11] = (wg.at[pl.ds(far, far), xr[1], 1], at_x(-1))
    c1_recv[10] = wg.at[pl.ds(0, far), xr[2], 1]
    c1_recv[11] = wg.at[pl.ds(far, far), xr[2], 1]
    c0_rows = [wg.at[yr[k], :, 0] for k in range(NY)]
    c1_rows = [wg.at[:, xr[k], 1] for k in range(NX)]

    def start0(*indices):
        for i in indices:
            w_copy(i, *c0_send[i]).start()

    def start1(*indices):
        for i in indices:
            w_copy(i, *c1_send[i]).start()

    def got0(*indices):
        for i in indices:
            w_copy(i, c0_recv[i], at_x(1)).wait_recv()

    def got1(*indices):
        for i in indices:
            w_copy(i, c1_recv[i], at_x(1)).wait_recv()

    def hand0(*indices):
        for i in indices:
            s_copy(i, c0_rows[i]).start()

    def hand1(*indices):
        for i in indices:
            s_copy(i, c1_rows[i]).start()

    def weights_stage(stage):
        @pl.when(core == 0)
        def _():
            if stage == 0:
                start0(0, 1)
            elif stage == 1:
                got0(0)
                start0(2)
                got0(1, 2)
                start0(3, 4)
                hand0(0)
            elif stage == 2:
                got0(3)
                start0(5)
                got0(4)
                start0(6)
                hand0(7, 1)
            elif stage == 3:
                got0(5)
                start0(7)
                got0(6)
                start0(8)
                hand0(6, 2)
            elif stage == 4:
                got0(7)
                start0(9)
                got0(8)
                start0(10)
                hand0(5, 3)
            else:
                got0(9, 10)
                hand0(4)
                for i in range(NX):
                    s_copy(i, c1_rows[i]).wait_recv()
                for i in range(11):
                    w_copy(i, *c0_send[i]).wait_send()
                for i in range(NY):
                    s_copy(i, c0_rows[i]).wait_send()

        @pl.when(core == 1)
        def _():
            if stage == 0:
                start1(0, 1)
            elif stage == 1:
                for r in range(3):
                    got1(2 * r)
                    start1(2 * r + 2)
                    got1(2 * r + 1)
                    start1(2 * r + 3)
                got1(6, 7)
                start1(8, 9)
                hand1(0)
            elif stage == 4:
                got1(8)
                start1(10)
                got1(9)
                start1(11)
                hand1(3, 1)
            elif stage == 5:
                got1(10, 11)
                hand1(2)
                for i in range(NY):
                    s_copy(i, c0_rows[i]).wait_recv()
                for i in range(12):
                    w_copy(i, *c1_send[i]).wait_send()
                for i in range(NX):
                    s_copy(i, c1_rows[i]).wait_send()

    own_sums(0)

    pl.semaphore_wait(barrier, len(partners))

    weights_stage(0)
    for direction in range(2):
        ag_copy(0, direction, 0).start()
    for d in range(1, nz):
        sums_copy(0, d).start()

    wm_copy.wait()
    angle = tstep.astype(F32) * tfreq_ref[...]
    emb = jnp.concatenate([jnp.cos(angle), jnp.sin(angle)], axis=1)
    high = emb.astype(BF16).astype(F32)
    middle = (emb - high).astype(BF16).astype(F32)
    low = (emb - high - middle).astype(BF16).astype(F32)
    index = lax.broadcasted_iota(jnp.int32, (16, TEMB), 0)
    parts = jnp.where(index == 0, high, jnp.where(index == 1, middle, jnp.where(index == 2, low, 0.0)))
    modg[z] = jnp.zeros((8, width), F32)
    for c in range(3):
        modul = jnp.dot(parts.astype(BF16), wm[c], preferred_element_type=F32)
        modg[z, c : c + 1, :] = jnp.sum(modul, axis=0, keepdims=True)

    def mod_copy(d):
        return remote(modg.at[z], modg.at[z], mod_send.at[d], mod_recv.at[d], at_z(d))

    def mod_arrival(d):
        k = ring(z, -d, nz)
        return remote(modg.at[k], modg.at[k], mod_send.at[d], mod_recv.at[d], at_z(d))

    for d in range(1, nz):
        mod_copy(d).start()

    acc[...] = jnp.zeros_like(acc)
    weights_stage(1)
    for d in range(1, nz):
        mod_arrival(d).wait_recv()

    for step in range(STEPS):
        if step > 0:
            for part in range(2):
                rows = pl.ds(part * half, half)
                sh_arrival = remote(
                    upd.at[0, part], xg.at[1, z, rows, :], sh_send.at[0, part], sh_recv.at[0, part], before
                )
                sh_arrival.wait_recv()

            @pl.when(last_slot)
            def _():
                noise_copy.wait()
                xg[1, z] = fresh[0:tokf]

            for direction in range(2):
                ag_copy(step, direction, 0).start()
            own_sums(step)
            for d in range(1, nz):
                sums_copy(step, d).start()
            acc[...] = jnp.zeros_like(acc)
        finish_sums(step)
        modulate(step, z)
        if step > 0:
            project(z)
        for r in range(nz // 2):
            for direction in range(2):
                ag_arrival(step, direction, r).wait_recv()
                if r < nz // 2 - 1:
                    ag_copy(step, direction, r + 1).start()
            blocks = [ring(z, -r - 1, nz), ring(z, r + 1, nz)] if r < nz // 2 - 1 else [ring(z, nz // 2, nz)]
            for k in blocks:
                modulate(step, k)
                if step > 0:
                    project(k)
            if step == 0:
                weights_stage(r + 2)
        if step == 0:

            def project_block(k, carry):
                project(k)
                return carry

            lax.fori_loop(0, nz, project_block, 0)

        for c in range(2):
            kv[step, c] = acc[:, (c + 1) * local_hh : (c + 2) * local_hh].astype(BF16)
            remote(kv.at[step, c], prev.at[step, c], kv_send.at[step, c], kv_recv.at[step, c], after).start()
        query[...] = acc[:, 0:local_hh].astype(BF16)

        def kv_arrival(c):
            return remote(kv.at[step, c], prev.at[step, c], kv_send.at[step, c], kv_recv.at[step, c], after)

        def scores(keys):
            s = lax.dot_general(
                query[:, keys[1]], keys[0][:, keys[1]], (((1,), (1,)), ((), ())), preferred_element_type=F32
            )
            return jnp.exp(s * (1.0 / math.sqrt(HD)))

        columns = [slice(i * HD, (i + 1) * HD) for i in range(heads)]
        own = [scores((kv.at[step, 0], columns[i])) for i in range(heads)]
        kv_arrival(0).wait_recv()
        behind = [
            jnp.where(q > 0, scores((prev.at[step, 0], columns[i])), 0.0) for i in range(heads)
        ]
        kv_arrival(1).wait_recv()
        for i in range(heads):
            total = jnp.sum(own[i], axis=1, keepdims=True) + jnp.sum(behind[i], axis=1, keepdims=True)
            p_own = (own[i] / total).astype(BF16)
            p_behind = (behind[i] / total).astype(BF16)
            out = jnp.dot(p_own, kv[step, 1, :, columns[i]], preferred_element_type=F32)
            out = out + jnp.dot(p_behind, prev[step, 1, :, columns[i]], preferred_element_type=F32)
            attn[:, columns[i]] = out.astype(BF16)

        if step == 0:
            for copy in wo_copies:
                copy.wait()

        def rs_term(direction, s):
            k = ring(z, -1 - s, nz) if direction == 0 else ring(z, 1 + s - nz, nz)
            rows = attn[direction * half : (direction + 1) * half, :]
            return jnp.dot(rows, wo[k], preferred_element_type=F32)

        def rs_copy(direction, s):
            return remote(
                rs_out.at[step, direction, s],
                rs_in.at[step, direction, s],
                rs_send.at[step, direction, s],
                rs_recv.at[step, direction, s],
                at_z(1 if direction == 0 else -1),
            )

        for direction in range(2):
            rs_out[step, direction, 0] = rs_term(direction, 0).astype(BF16)
            rs_copy(direction, 0).start()

        def hop(s, carry):
            terms = [rs_term(direction, s) for direction in range(2)]
            for direction in range(2):
                rs_copy(direction, s - 1).wait_recv()
                rs_out[step, direction, s] = (rs_in[step, direction, s - 1].astype(F32) + terms[direction]).astype(BF16)
                rs_copy(direction, s).start()
            return carry

        lax.fori_loop(1, nz - 1, hop, 0)
        terms = [rs_term(direction, nz - 1) for direction in range(2)]
        gate = modg[z][2:3]
        for direction in range(2):
            rows = slice(direction * half, (direction + 1) * half)
            rs_copy(direction, nz - 2).wait_recv()
            summed = rs_in[step, direction, nz - 2].astype(F32) + terms[direction]
            vel = gate * summed
            if step == STEPS - 1:
                vel_ref[rows, :] = vel.astype(BF16)
            upd[step, direction] = (xg[step, z, rows, :].astype(F32) + sig_step * vel).astype(BF16)
            if step < STEPS - 1:
                target = xg.at[step + 1, z, pl.ds(direction * half, half), :]
            else:
                target = new_ref.at[pl.ds(direction * half, half), :]
            remote(upd.at[step, direction], target, sh_send.at[step, direction], sh_recv.at[step, direction], before).start()

    for part in range(2):
        remote(
            upd.at[1, part], new_ref.at[pl.ds(part * half, half), :], sh_send.at[1, part], sh_recv.at[1, part], before
        ).wait_recv()

    @pl.when(last_slot)
    def _():
        new_ref[...] = fresh[tokf : 2 * tokf]

    for d in range(1, nz):
        mod_copy(d).wait_send()
    for step in range(STEPS):
        for d in range(1, nz):
            sums_copy(step, d).wait_send()
        for direction in range(2):
            for r in range(nz // 2):
                ag_copy(step, direction, r).wait_send()
            for s in range(nz - 1):
                remote(
                    rs_out.at[step, direction, s],
                    rs_in.at[step, direction, s],
                    rs_send.at[step, direction, s],
                    rs_recv.at[step, direction, s],
                    at_z(1 if direction == 0 else -1),
                ).wait_send()
            remote(
                upd.at[step, direction], upd.at[step, direction], sh_send.at[step, direction], sh_recv.at[step, direction], before
            ).wait_send()
        for c in range(2):
            remote(kv.at[step, c], prev.at[step, c], kv_send.at[step, c], kv_recv.at[step, c], after).wait_send()


def solution(mesh):
    queue_len, nz = mesh.shape["queue"], mesh.shape["head"]

    def shards(states, noise, w_qkv, w_out, w_mod, sigma_table, timesteps, frame_index):
        tokf, width = states.shape
        rows = w_qkv.shape[0]
        local_hh = w_out.shape[0]
        half = tokf // 2
        full = width * nz
        freq = frequencies(full // 2)
        pfreq = jnp.asarray(np.concatenate([freq, freq]).reshape(nz, width))
        tfreq = jnp.asarray(frequencies(TEMB // 2).reshape(1, TEMB // 2))
        vmem = pl.BlockSpec(memory_space=pltpu.VMEM)
        smem = pl.BlockSpec(memory_space=pltpu.SMEM)
        anywhere = pl.BlockSpec(memory_space=pl.ANY)
        dma = pltpu.SemaphoreType.DMA
        hops = nz // 2
        return pl.pallas_call(
            functools.partial(kernel, queue_len, nz),
            out_shape=(
                jax.ShapeDtypeStruct((tokf, width), BF16),
                jax.ShapeDtypeStruct((tokf, width), BF16),
            ),
            in_specs=[smem, smem, smem, vmem, vmem, vmem, vmem, anywhere, anywhere, anywhere],
            out_specs=(vmem, vmem),
            scratch_shapes=[
                pltpu.VMEM((STEPS, nz, tokf, width), BF16),
                pltpu.VMEM((nz, tokf, width), BF16),
                pltpu.VMEM((NY, NX, CORES, rows, 3 * local_hh), BF16),
                pltpu.VMEM((nz, local_hh, width), BF16),
                pltpu.VMEM((3, TEMB, width), BF16),
                pltpu.VMEM((tokf, 3 * local_hh), F32),
                pltpu.VMEM((tokf, local_hh), BF16),
                pltpu.VMEM((STEPS, 2, tokf, local_hh), BF16),
                pltpu.VMEM((STEPS, 2, tokf, local_hh), BF16),
                pltpu.VMEM((tokf, local_hh), BF16),
                pltpu.VMEM((STEPS, 2, nz - 1, half, width), BF16),
                pltpu.VMEM((STEPS, 2, nz - 1, half, width), BF16),
                pltpu.VMEM((STEPS, 2, half, width), BF16),
                pltpu.VMEM((STEPS * tokf, width), BF16),
                pltpu.VMEM((STEPS, nz, width), F32),
                pltpu.VMEM((STEPS, nz, 8, tokf), F32),
                pltpu.VMEM((nz, 8, width), F32),
                pltpu.VMEM((tokf, LANES), F32),
                pltpu.VMEM((tokf, LANES), F32),
                dma((nz,)),
                dma,
                dma,
                dma((STEPS, 2, hops)),
                dma((STEPS, 2, hops)),
                dma((12,)),
                dma((12,)),
                dma((NY,)),
                dma((NY,)),
                dma((STEPS, nz)),
                dma((STEPS, nz)),
                dma((nz,)),
                dma((nz,)),
                dma((STEPS, 2)),
                dma((STEPS, 2)),
                dma((STEPS, 2, nz - 1)),
                dma((STEPS, 2, nz - 1)),
                dma((STEPS, 2)),
                dma((STEPS, 2)),
            ],
            compiler_params=pltpu.CompilerParams(
                collective_id=0, has_side_effects=True, vmem_limit_bytes=48 * 1024 * 1024
            ),
        )(
            sigma_table,
            timesteps,
            frame_index,
            pfreq,
            tfreq,
            states,
            jnp.transpose(w_qkv, (1, 0, 2)),
            jnp.transpose(w_mod, (1, 0, 2)),
            w_out,
            noise,
        )

    in_specs = (
        P("queue", "head"),
        P(None, "head"),
        P("queue", None, "head"),
        P("head", None),
        P(None, None, "head"),
        P(),
        P(),
        P(),
    )
    out_specs = (P("queue", "head"), P("queue", "head"))
    return jax.shard_map(shards, mesh=mesh, in_specs=in_specs, out_specs=out_specs, check_vma=False)
```

time: 375 us -> 176 us (0.47)
  the two profiles are of different devices: /device:TPU:31 before, /device:TPU:63 now
where the time goes in v1:
time: 176 us; the launch traced here: 175 us
  Pallas kernels  165 us (94%)
  local copies, waits for them, and re-layouts  10.3 us (6%)
    pallas_call x1, Pallas kernels, shards(): pl.pallas_call(functools.partial(kernel, queue_len, nz), out_shape=(jax.S...  165 us
    unnamed x22, local copies, waits for them, and re-layouts  10.3 us

profile of v1, /device:TPU:63, one launch (start us, length us, event | category | flops | bytes accessed | tf_op | source)
XLA Modules:
  0.0 175.4 jit_solution(15533767482859665224)
XLA Ops:
  0.6 0.0 copy-start
  0.6 1.7 copy-done
  2.3 0.0 copy-start.1
  2.3 1.1 copy-done.1
  3.4 0.0 copy-start.2
  3.4 1.0 copy-done.2
  4.4 0.0 copy-start.3
  4.4 0.9 copy-done.3
  5.3 0.0 copy-start.4
  5.3 0.9 copy-done.4
  6.2 0.0 copy-start.5
  6.2 0.7 copy-done.5
  6.9 0.0 copy-start.6
  6.9 0.7 copy-done.6
  7.6 0.0 copy-start.7
  7.6 0.7 copy-done.7
  8.2 0.0 copy-start.8
  8.2 0.7 copy-done.8
  8.9 0.0 copy-start.9
  8.9 0.7 copy-done.9
  9.5 164.5 %shard_map.113 = (bf16[256,384]{1,0:T(8,128)(2,1)S(1)}, bf16[256,384]{1,0:T(8,128)(2,1)S(1)}) custom-call(f32[1000]{0:T(1024)S(1)} %copy-done.6, s32[64]{0:T(128)S(1)} %copy-done.7, s32[64]{0:T(128)S(1)} %copy-done.8, f32[8,384]{1,0:T(8,128)S(1)} %copy-done.5, f32[1,128]{1,0:T(1,128)S(1)} %copy-done.9, bf16[256,384]{1,0:T(8,128)(2,1)S(1)} %copy-done.3, ...), custom_call_target="tpu_custom_call" | custom-call | tf_op jit(solution)/shard_map/pallas_call | solution.py:578
  174.1 0.7 copy.14
  174.8 0.7 copy.15
Async XLA Ops:
  0.6 1.7 copy-start
  2.3 1.1 copy-start.1
  3.4 1.0 copy-start.2
  4.4 0.9 copy-start.3
  5.3 0.9 copy-start.4
  6.2 0.7 copy-start.5
  6.9 0.7 copy-start.6
  7.6 0.7 copy-start.7
  8.2 0.7 copy-start.8
  8.9 0.7 copy-start.9

commit v2 on v1

v2 whole, which is shorter than its diff:
```python
import functools
import math

import jax
import jax.numpy as jnp
import numpy as np
from jax import lax
from jax.experimental import pallas as pl
from jax.experimental.pallas import tpu as pltpu
from jax.sharding import PartitionSpec as P

MESH = pl.DeviceIdType.MESH
HD = 128
TEMB = 256
STEPS = 2
NX = 4
NY = 8
CORES = 2
AG_PARTS = 4
RS_PARTS = 4
LANES = 128
F32 = jnp.float32
BF16 = jnp.bfloat16


def frequencies(half):
    return np.exp(-np.log(10000.0) * np.arange(half) / half).astype(np.float32)


def kernel(
    queue_len,
    nz,
    sigma_hbm,
    tsteps_hbm,
    frames_hbm,
    pfreq_hbm,
    tfreq_hbm,
    states_hbm,
    wq_hbm,
    wm_hbm,
    wo_hbm,
    noise_hbm,
    new_ref,
    vel_ref,
    xg,
    h,
    wg,
    wo,
    wm,
    acc,
    query,
    kv,
    prev,
    attn,
    rs_out,
    rs_in,
    upd,
    term,
    fresh,
    pos,
    sg,
    modg,
    mean_b,
    rstd_b,
    sigma_ref,
    tsteps_ref,
    frames_ref,
    pfreq_ref,
    tfreq_ref,
    in_sem,
    wo_sem,
    wm_sem,
    noise_sem,
    ag_send,
    ag_recv,
    w_send,
    w_recv,
    s_send,
    s_recv,
    st_send,
    st_recv,
    mod_send,
    mod_recv,
    kv_send,
    kv_recv,
    rs_send,
    rs_recv,
    sh_send,
    sh_recv,
):
    q = lax.axis_index("queue")
    z = lax.axis_index("head")
    core = lax.rem(q, CORES)
    x = lax.rem(q // CORES, NX)
    y = q // (CORES * NX)
    tokf, width = states_hbm.shape
    half = tokf // 2
    full = width * nz
    tiles = width // LANES
    local_hh = wo.shape[1]
    heads = local_hh // HD

    def ring(base, offset, size):
        return lax.rem(base + offset + size, size)

    def queue_id(yy, xx, cc):
        return (yy * NX + xx) * CORES + cc

    def at_z(offset):
        return (q, ring(z, offset, nz))

    def at_x(offset):
        return (queue_id(y, ring(x, offset, NX), core), z)

    def at_y(offset):
        return (queue_id(ring(y, offset, NY), x, core), z)

    sibling = (queue_id(y, x, 1 - core), z)
    after = (ring(q, 1, queue_len), z)
    before = (ring(q, -1, queue_len), z)
    last_slot = q == queue_len - 1

    def remote(src, dst, send, recv, device):
        return pltpu.make_async_remote_copy(
            src_ref=src, dst_ref=dst, send_sem=send, recv_sem=recv, device_id=device, device_id_type=MESH
        )

    scalar_copies = [
        pltpu.make_async_copy(src, dst, in_sem.at[i])
        for i, (src, dst) in enumerate(
            [
                (tsteps_hbm, tsteps_ref),
                (frames_hbm, frames_ref),
                (sigma_hbm, sigma_ref),
                (pfreq_hbm, pfreq_ref),
                (tfreq_hbm, tfreq_ref),
            ]
        )
    ]
    states_copy = pltpu.make_async_copy(states_hbm, xg.at[0, z], in_sem.at[5])
    wq_copies = [
        pltpu.make_async_copy(
            wq_hbm.at[c], wg.at[y, x, core, :, c * local_hh : (c + 1) * local_hh], in_sem.at[6 + c]
        )
        for c in range(3)
    ]
    states_copy.start()
    for copy in wq_copies + scalar_copies:
        copy.start()

    barrier = pltpu.get_barrier_semaphore()
    partners = [at_z(d) for d in range(1, nz)]
    partners += [at_x(1), at_x(-1), at_y(1), at_y(-1), sibling, after, before]
    for partner in partners:
        pl.semaphore_signal(barrier, inc=1, device_id=partner, device_id_type=MESH)

    wm_copy = pltpu.make_async_copy(wm_hbm, wm, wm_sem)
    wm_copy.start()
    wo_copies = [
        pltpu.make_async_copy(wo_hbm.at[:, b * width : (b + 1) * width], wo.at[b], wo_sem.at[b]) for b in range(nz)
    ]
    for copy in wo_copies:
        copy.start()
    noise_copy = pltpu.make_async_copy(noise_hbm, fresh, noise_sem)

    @pl.when(last_slot)
    def _():
        noise_copy.start()

    for copy in scalar_copies:
        copy.wait()

    tstep = tsteps_ref[q]
    sig_now = sigma_ref[tstep]
    sig_before = sigma_ref[tsteps_ref[jnp.maximum(q - 1, 0)]]
    sig_step = jnp.where(q > 0, sig_before, 0.0) - sig_now
    last_frame = frames_ref[queue_len - 1]

    block = lax.broadcasted_iota(jnp.int32, (nz, width), 0)
    for step in range(STEPS):
        ahead = q + step
        frame = jnp.where(
            ahead < queue_len, frames_ref[jnp.minimum(ahead, queue_len - 1)], last_frame + ahead - queue_len + 1
        )
        angle = frame.astype(F32) * pfreq_ref[...]
        pos[step] = jnp.where(block < nz // 2, jnp.sin(angle), jnp.cos(angle))

    def lanes(t):
        return slice(t * LANES, (t + 1) * LANES)

    def own_sums(step):
        row = pos[step, pl.ds(z, 1), :]
        sums = jnp.zeros((tokf, LANES), F32)
        squares = jnp.zeros((tokf, LANES), F32)
        for t in range(tiles):
            u = xg[step, z, :, lanes(t)].astype(F32) + row[:, lanes(t)]
            sums = sums + u
            squares = squares + u * u
        sums = jnp.sum(sums, axis=1, keepdims=True)
        squares = jnp.sum(squares, axis=1, keepdims=True)
        lane = lax.broadcasted_iota(jnp.int32, (tokf, LANES), 1)
        both = jnp.where(lane == 0, sums, jnp.where(lane == 1, squares, 0.0))
        sg[step, z] = both.T[0:8]

    def sums_copy(step, d):
        return remote(sg.at[step, z], sg.at[step, z], st_send.at[step, d], st_recv.at[step, d], at_z(d))

    def sums_arrival(step, d):
        k = ring(z, -d, nz)
        return remote(sg.at[step, k], sg.at[step, k], st_send.at[step, d], st_recv.at[step, d], at_z(d))

    def finish_sums(step):
        for d in range(1, nz):
            sums_arrival(step, d).wait_recv()
        total = sg[step, 0]
        for k in range(1, nz):
            total = total + sg[step, k]
        mean = total[0:1] / full
        var = total[1:2] / full - mean * mean
        rstd = lax.rsqrt(var + 1e-06)
        mean_b[...] = jnp.broadcast_to(mean, (LANES, tokf)).T
        rstd_b[...] = jnp.broadcast_to(rstd, (LANES, tokf)).T

    last_hop = nz // 2 - 1
    part_rows = tokf // AG_PARTS

    def ag_goes(direction, r, part):
        return r < last_hop or part // (AG_PARTS // 2) == direction

    def ag_remote(step, direction, r, part, k):
        ref = xg.at[step, k, pl.ds(part * part_rows, part_rows), :]
        return remote(
            ref,
            ref,
            ag_send.at[step, direction, r, part],
            ag_recv.at[step, direction, r, part],
            at_z(1 if direction == 0 else -1),
        )

    def ag_copy(step, direction, r, part):
        return ag_remote(step, direction, r, part, ring(z, -r if direction == 0 else r, nz))

    def ag_arrival(step, direction, r, part):
        return ag_remote(step, direction, r, part, ring(z, -r - 1 if direction == 0 else r + 1, nz))

    def ag_forward(step, r, part):
        for direction in range(2):
            if ag_goes(direction, r, part):
                ag_arrival(step, direction, r, part).wait_recv()
                if r < last_hop and ag_goes(direction, r + 1, part):
                    ag_copy(step, direction, r + 1, part).start()

    def modulate(step, k):
        row = pos[step, pl.ds(k, 1), :]
        rows = modg[k]
        shift, scale = rows[0:1], 1.0 + rows[1:2]
        for t in range(tiles):
            u = xg[step, k, :, lanes(t)].astype(F32) + row[:, lanes(t)]
            normed = (u - mean_b[...]) * rstd_b[...]
            h[k, :, lanes(t)] = (normed * scale[:, lanes(t)] + shift[:, lanes(t)]).astype(BF16)

    def project(k):
        weights = wg[k].reshape(width, 3 * local_hh)
        acc[...] += jnp.dot(h[k], weights, preferred_element_type=F32)

    near_x = (0, 3, 1, 2)
    near_y = (0, 1, 7, 2, 6, 3, 5, 4)
    far = NY // 2

    def piece(c, dy, dx):
        return wg.at[ring(y, dy, NY), ring(x, dx, NX), c]

    def w_remote(index, ref, device):
        return remote(ref, ref, w_send.at[index], w_recv.at[index], device)

    def s_remote(c, dy, dx):
        index = near_y.index(dy) * NX + near_x.index(dx)
        ref = piece(c, dy, dx)
        return remote(ref, ref, s_send.at[index], s_recv.at[index], sibling)

    def both_x(dx):
        return at_x(1) if dx == 0 else at_x(-1)

    def both_y(direction):
        return at_y(1 if direction == 0 else -1)

    def c0_index(r, direction, i):
        return 3 + (r * 2 + direction) * NX + i

    def c0_goes(r, direction, i):
        return r < far - 1 or i % 2 == direction

    def c0_dy(r, direction):
        return (-r if direction == 0 else r) % NY

    def c0_y_copy(r, direction, i):
        return w_remote(c0_index(r, direction, i), piece(0, c0_dy(r, direction), near_x[i]), both_y(direction))

    def c0_y_arrival(r, direction, i):
        return w_remote(c0_index(r, direction, i), piece(0, c0_dy(r + 1, direction), near_x[i]), both_y(direction))

    def c0_row(i):
        for direction in range(2):
            c0_y_copy(0, direction, i).start()
        s_remote(0, 0, near_x[i]).start()

    def c0_x_copies():
        return [
            w_remote(0, piece(0, 0, 0), at_x(1)),
            w_remote(1, piece(0, 0, 0), at_x(-1)),
            w_remote(2, piece(0, 0, 3), at_x(1)),
        ]

    def c0_start():
        copies = c0_x_copies()
        copies[0].start()
        copies[1].start()
        c0_row(0)

    def c0_first_x():
        w_remote(0, piece(0, 0, 3), at_x(1)).wait_recv()
        c0_x_copies()[2].start()
        c0_row(1)
        w_remote(1, piece(0, 0, 1), at_x(-1)).wait_recv()
        c0_row(2)

    def c0_second_x():
        w_remote(2, piece(0, 0, 2), at_x(1)).wait_recv()
        c0_row(3)

    def c0_y(r, i):
        def event():
            for direction in range(2):
                if c0_goes(r, direction, i):
                    c0_y_arrival(r, direction, i).wait_recv()
                    if r < far - 1 and c0_goes(r + 1, direction, i):
                        c0_y_copy(r + 1, direction, i).start()
                    s_remote(0, c0_dy(r + 1, direction), near_x[i]).start()

        return event

    def c1_y_part(r, direction, dy):
        ref = piece(1, dy, 0)
        if r == far - 1:
            ref = ref.at[pl.ds(0, 32)] if direction == 0 else ref.at[pl.ds(32, 16)]
        return ref

    def c1_y_copy(r, direction):
        return w_remote(2 * r + direction, c1_y_part(r, direction, c0_dy(r, direction)), both_y(direction))

    def c1_y_arrival(r, direction):
        return w_remote(2 * r + direction, c1_y_part(r, direction, c0_dy(r + 1, direction)), both_y(direction))

    def c1_first(n, direction, dx):
        return w_remote(8 + direction * NY + n, piece(1, near_y[n], dx), at_x(1 if direction == 0 else -1))

    def c1_second(n, dx):
        return w_remote(24 + n, piece(1, near_y[n], dx), at_x(1 if n % 2 == 0 else -1))

    def c1_column(n):
        for direction in range(2):
            c1_first(n, direction, 0).start()
        s_remote(1, near_y[n], 0).start()

    def c1_start():
        for direction in range(2):
            c1_y_copy(0, direction).start()
        c1_column(0)

    def c1_y(r):
        def event():
            for direction in range(2):
                c1_y_arrival(r, direction).wait_recv()
                if r < far - 1:
                    c1_y_copy(r + 1, direction).start()
            if r < far - 1:
                c1_column(2 * r + 1)
                c1_column(2 * r + 2)
            else:
                c1_column(NY - 1)

        return event

    def c1_x(n):
        def event():
            c1_first(n, 0, 3).wait_recv()
            if n % 2 == 0:
                c1_second(n, 3).start()
            c1_first(n, 1, 1).wait_recv()
            if n % 2 == 1:
                c1_second(n, 1).start()
            s_remote(1, near_y[n], 3).start()
            s_remote(1, near_y[n], 1).start()

        return event

    def c1_xx(n):
        def event():
            c1_second(n, 2).wait_recv()
            s_remote(1, near_y[n], 2).start()

        return event

    c0_events = [[c0_first_x], [c0_y(0, 0)], [c0_second_x, c0_y(0, 1)], [c0_y(0, 2), c0_y(0, 3)]]
    c0_events += [[c0_y(r, i)] for r in range(1, far) for i in range(NX)]
    c1_events = [
        [c1_y(0)],
        [c1_x(0)],
        [c1_y(1)],
        [c1_x(1), c1_x(2)],
        [c1_xx(0)],
        [c1_y(2)],
        [c1_x(3), c1_x(4)],
        [c1_xx(1), c1_xx(2)],
        [c1_y(3)],
        [c1_x(5), c1_x(6)],
        [c1_xx(3)],
        [c1_xx(4)],
        [c1_x(7)],
        [c1_xx(5)],
        [c1_xx(6)],
        [c1_xx(7)],
    ]

    def weights_events(slot):
        @pl.when(core == 0)
        def _():
            for event in c0_events[slot]:
                event()

        @pl.when(core == 1)
        def _():
            for event in c1_events[slot]:
                event()

    def from_sibling(n):
        for c in range(CORES):

            @pl.when(core != c)
            def _():
                for dx in near_x:
                    s_remote(c, near_y[n], dx).wait_recv()

    def weights_drain():
        @pl.when(core == 0)
        def _():
            for copy in c0_x_copies():
                copy.wait_send()
            for r in range(far):
                for direction in range(2):
                    for i in range(NX):
                        if c0_goes(r, direction, i):
                            c0_y_copy(r, direction, i).wait_send()

        @pl.when(core == 1)
        def _():
            for r in range(far):
                for direction in range(2):
                    c1_y_copy(r, direction).wait_send()
            for n in range(NY):
                for direction in range(2):
                    c1_first(n, direction, 0).wait_send()
                c1_second(n, 3 if n % 2 == 0 else 1).wait_send()

        for c in range(CORES):

            @pl.when(core == c)
            def _():
                for dy in near_y:
                    for dx in near_x:
                        s_remote(c, dy, dx).wait_send()

    rs_rows = tokf // RS_PARTS

    def rows_of(part):
        return pl.ds(part * rs_rows, rs_rows)

    def rs_goes(direction, s, part):
        return s > 0 or part // (RS_PARTS // 2) == direction

    def rs_remote(step, direction, s, part):
        rows = rows_of(part)
        return remote(
            rs_out.at[step, direction, s, rows, :],
            rs_in.at[step, direction, s, rows, :],
            rs_send.at[step, direction, s, part],
            rs_recv.at[step, direction, s, part],
            at_z(1 if direction == 0 else -1),
        )

    def sh_copy(step, part):
        rows = rows_of(part)
        return remote(
            upd.at[step, rows, :],
            new_ref.at[rows, :] if step == STEPS - 1 else xg.at[step + 1, z, rows, :],
            sh_send.at[step, part],
            sh_recv.at[step, part],
            before,
        )

    sh_arrival = sh_copy

    states_copy.wait()
    own_sums(0)
    for copy in wq_copies:
        copy.wait()

    pl.semaphore_wait(barrier, len(partners))

    for d in range(1, nz):
        sums_copy(0, d).start()
    pl.when(core == 0)(c0_start)
    pl.when(core == 1)(c1_start)
    for part in range(AG_PARTS):
        for direction in range(2):
            ag_copy(0, direction, 0, part).start()

    wm_copy.wait()
    angle = tstep.astype(F32) * tfreq_ref[...]
    emb = jnp.concatenate([jnp.cos(angle), jnp.sin(angle)], axis=1)
    high = emb.astype(BF16).astype(F32)
    middle = (emb - high).astype(BF16).astype(F32)
    low = (emb - high - middle).astype(BF16).astype(F32)
    index = lax.broadcasted_iota(jnp.int32, (16, TEMB), 0)
    parts = jnp.where(index == 0, high, jnp.where(index == 1, middle, jnp.where(index == 2, low, 0.0)))
    modg[z] = jnp.zeros((8, width), F32)
    for c in range(3):
        modul = jnp.dot(parts.astype(BF16), wm[c], preferred_element_type=F32)
        modg[z, c : c + 1, :] = jnp.sum(modul, axis=0, keepdims=True)

    def mod_copy(d):
        return remote(modg.at[z], modg.at[z], mod_send.at[d], mod_recv.at[d], at_z(d))

    def mod_arrival(d):
        k = ring(z, -d, nz)
        return remote(modg.at[k], modg.at[k], mod_send.at[d], mod_recv.at[d], at_z(d))

    for d in range(1, nz):
        mod_copy(d).start()

    acc[...] = jnp.zeros_like(acc)
    for step in range(STEPS):
        if step > 0:
            @pl.when(jnp.logical_not(last_slot))
            def _():
                for part in range(RS_PARTS):
                    sh_arrival(0, part).wait_recv()

            @pl.when(last_slot)
            def _():
                noise_copy.wait()
                xg[1, z] = fresh[0:tokf]

            own_sums(step)
            for d in range(1, nz):
                sums_copy(step, d).start()
            for part in range(AG_PARTS):
                for direction in range(2):
                    ag_copy(step, direction, 0, part).start()
            acc[...] = jnp.zeros_like(acc)
        ready = [z]
        formed = False
        for r in range(nz // 2):
            for part in range(AG_PARTS):
                ag_forward(step, r, part)
                if step == 0 and r < last_hop:
                    weights_events(r * AG_PARTS + part)
                if (r, part) == ((nz // 2 - 2, 0) if step == 0 else (0, 0)):
                    formed = True
                    if step == 0:
                        for d in range(1, nz):
                            mod_arrival(d).wait_recv()
                    finish_sums(step)
                if ready and formed and (step == 0 or part % 2 == 1):
                    k = ready.pop(0)
                    modulate(step, k)
                    if step > 0:
                        project(k)
            ready += [ring(z, -r - 1, nz), ring(z, r + 1, nz)] if r < last_hop else [ring(z, nz // 2, nz)]
        for k in ready:
            modulate(step, k)
            if step > 0:
                project(k)
        if step == 0:
            for part in range(AG_PARTS):
                weights_events(last_hop * AG_PARTS + part)
                for n in ((0, 1), (2,), (3,), (4,))[part]:
                    from_sibling(n)
                    project(ring(y, near_y[n], NY))
            for n in range(5, NY):
                from_sibling(n)
                project(ring(y, near_y[n], NY))

        for c in range(2):
            kv[step, c] = acc[:, (c + 1) * local_hh : (c + 2) * local_hh].astype(BF16)
            remote(kv.at[step, c], prev.at[step, c], kv_send.at[step, c], kv_recv.at[step, c], after).start()
        query[...] = acc[:, 0:local_hh].astype(BF16)

        def kv_arrival(c):
            return remote(kv.at[step, c], prev.at[step, c], kv_send.at[step, c], kv_recv.at[step, c], after)

        def scores(keys):
            s = lax.dot_general(
                query[:, keys[1]], keys[0][:, keys[1]], (((1,), (1,)), ((), ())), preferred_element_type=F32
            )
            return jnp.exp(s * (1.0 / math.sqrt(HD)))

        columns = [slice(i * HD, (i + 1) * HD) for i in range(heads)]
        own = [scores((kv.at[step, 0], columns[i])) for i in range(heads)]
        kv_arrival(0).wait_recv()
        behind = [
            jnp.where(q > 0, scores((prev.at[step, 0], columns[i])), 0.0) for i in range(heads)
        ]
        kv_arrival(1).wait_recv()
        for i in range(heads):
            total = jnp.sum(own[i], axis=1, keepdims=True) + jnp.sum(behind[i], axis=1, keepdims=True)
            p_own = (own[i] / total).astype(BF16)
            p_behind = (behind[i] / total).astype(BF16)
            out = jnp.dot(p_own, kv[step, 1, :, columns[i]], preferred_element_type=F32)
            out = out + jnp.dot(p_behind, prev[step, 1, :, columns[i]], preferred_element_type=F32)
            attn[:, columns[i]] = out.astype(BF16)

        if step == 0:
            for copy in wo_copies:
                copy.wait()

        def rs_term(direction, s, first, count):
            k = ring(z, nz // 2 - s if direction == 0 else s - nz // 2, nz)
            return jnp.dot(attn[first : first + count, :], wo[k], preferred_element_type=F32)

        for s in range(2):
            for direction in range(2):
                side = direction if s == 0 else 1 - direction
                rs_out[step, direction, s, side * half : (side + 1) * half, :] = rs_term(
                    direction, s, side * half, half
                ).astype(BF16)
                for part in range(RS_PARTS):
                    if part // (RS_PARTS // 2) == side:
                        rs_remote(step, direction, s, part).start()
        for s in range(1, nz // 2):
            for direction in range(2):
                if s == 1:
                    rows = slice(direction * half, (direction + 1) * half)
                    term[direction, rows, :] = rs_term(direction, s, direction * half, half)
                else:
                    term[direction] = rs_term(direction, s, 0, tokf)
            for i in range(RS_PARTS):
                for direction in range(2):
                    part = (i + RS_PARTS // 2 * (1 - direction)) % RS_PARTS
                    if rs_goes(direction, s - 1, part):
                        rows = rows_of(part)
                        rs_remote(step, direction, s - 1, part).wait_recv()
                        rs_out[step, direction, s, rows, :] = (
                            rs_in[step, direction, s - 1, rows, :].astype(F32) + term[direction, rows, :]
                        ).astype(BF16)
                        rs_remote(step, direction, s, part).start()
        term[0] = rs_term(0, nz // 2, 0, tokf)
        gate = modg[z][2:3]
        for part in (2, 0, 3, 1):
            rows = rows_of(part)
            summed = term[0, rows, :]
            for direction in range(2):
                rs_remote(step, direction, nz // 2 - 1, part).wait_recv()
                summed = summed + rs_in[step, direction, nz // 2 - 1, rows, :].astype(F32)
            vel = gate * summed
            if step == STEPS - 1:
                vel_ref[rows, :] = vel.astype(BF16)
            upd[step, rows, :] = (xg[step, z, rows, :].astype(F32) + sig_step * vel).astype(BF16)

            @pl.when(q > 0)
            def _():
                sh_copy(step, part).start()

    @pl.when(last_slot)
    def _():
        new_ref[...] = fresh[tokf : 2 * tokf]

    @pl.when(jnp.logical_not(last_slot))
    def _():
        for part in range(RS_PARTS):
            sh_arrival(1, part).wait_recv()

    weights_drain()
    for d in range(1, nz):
        mod_copy(d).wait_send()
    for step in range(STEPS):
        for d in range(1, nz):
            sums_copy(step, d).wait_send()
        for direction in range(2):
            for part in range(AG_PARTS):
                for r in range(nz // 2):
                    if ag_goes(direction, r, part):
                        ag_copy(step, direction, r, part).wait_send()
            for part in range(RS_PARTS):
                for hop in range(nz // 2):
                    if rs_goes(direction, hop, part):
                        rs_remote(step, direction, hop, part).wait_send()
        for c in range(2):
            remote(kv.at[step, c], prev.at[step, c], kv_send.at[step, c], kv_recv.at[step, c], after).wait_send()

    @pl.when(q > 0)
    def _():
        for step in range(STEPS):
            for part in range(RS_PARTS):
                sh_copy(step, part).wait_send()


def solution(mesh):
    queue_len, nz = mesh.shape["queue"], mesh.shape["head"]

    def shards(states, noise, w_qkv, w_out, w_mod, sigma_table, timesteps, frame_index):
        tokf, width = states.shape
        rows = w_qkv.shape[0]
        local_hh = w_out.shape[0]
        full = width * nz
        freq = frequencies(full // 2)
        pfreq = jnp.asarray(np.concatenate([freq, freq]).reshape(nz, width))
        tfreq = jnp.asarray(frequencies(TEMB // 2).reshape(1, TEMB // 2))
        vmem = pl.BlockSpec(memory_space=pltpu.VMEM)
        anywhere = pl.BlockSpec(memory_space=pl.ANY)
        dma = pltpu.SemaphoreType.DMA
        hops = nz // 2
        return pl.pallas_call(
            functools.partial(kernel, queue_len, nz),
            out_shape=(
                jax.ShapeDtypeStruct((tokf, width), BF16),
                jax.ShapeDtypeStruct((tokf, width), BF16),
            ),
            in_specs=[anywhere] * 10,
            out_specs=(vmem, vmem),
            scratch_shapes=[
                pltpu.VMEM((STEPS, nz, tokf, width), BF16),
                pltpu.VMEM((nz, tokf, width), BF16),
                pltpu.VMEM((NY, NX, CORES, rows, 3 * local_hh), BF16),
                pltpu.VMEM((nz, local_hh, width), BF16),
                pltpu.VMEM((3, TEMB, width), BF16),
                pltpu.VMEM((tokf, 3 * local_hh), F32),
                pltpu.VMEM((tokf, local_hh), BF16),
                pltpu.VMEM((STEPS, 2, tokf, local_hh), BF16),
                pltpu.VMEM((STEPS, 2, tokf, local_hh), BF16),
                pltpu.VMEM((tokf, local_hh), BF16),
                pltpu.VMEM((STEPS, 2, hops, tokf, width), BF16),
                pltpu.VMEM((STEPS, 2, hops, tokf, width), BF16),
                pltpu.VMEM((STEPS, tokf, width), BF16),
                pltpu.VMEM((2, tokf, width), F32),
                pltpu.VMEM((STEPS * tokf, width), BF16),
                pltpu.VMEM((STEPS, nz, width), F32),
                pltpu.VMEM((STEPS, nz, 8, tokf), F32),
                pltpu.VMEM((nz, 8, width), F32),
                pltpu.VMEM((tokf, LANES), F32),
                pltpu.VMEM((tokf, LANES), F32),
                pltpu.SMEM(sigma_table.shape, F32),
                pltpu.SMEM(timesteps.shape, jnp.int32),
                pltpu.SMEM(frame_index.shape, jnp.int32),
                pltpu.VMEM(pfreq.shape, F32),
                pltpu.VMEM(tfreq.shape, F32),
                dma((9,)),
                dma((nz,)),
                dma,
                dma,
                dma((STEPS, 2, hops, AG_PARTS)),
                dma((STEPS, 2, hops, AG_PARTS)),
                dma((35,)),
                dma((35,)),
                dma((NY * NX,)),
                dma((NY * NX,)),
                dma((STEPS, nz)),
                dma((STEPS, nz)),
                dma((nz,)),
                dma((nz,)),
                dma((STEPS, 2)),
                dma((STEPS, 2)),
                dma((STEPS, 2, hops, RS_PARTS)),
                dma((STEPS, 2, hops, RS_PARTS)),
                dma((STEPS, RS_PARTS)),
                dma((STEPS, RS_PARTS)),
            ],
            compiler_params=pltpu.CompilerParams(
                collective_id=0, has_side_effects=True, vmem_limit_bytes=60 * 1024 * 1024
            ),
        )(
            sigma_table,
            timesteps,
            frame_index,
            pfreq,
            tfreq,
            states,
            jnp.transpose(w_qkv, (1, 0, 2)),
            jnp.transpose(w_mod, (1, 0, 2)),
            w_out,
            noise,
        )

    in_specs = (
        P("queue", "head"),
        P(None, "head"),
        P("queue", None, "head"),
        P("head", None),
        P(None, None, "head"),
        P(),
        P(),
        P(),
    )
    out_specs = (P("queue", "head"), P("queue", "head"))
    return jax.shard_map(shards, mesh=mesh, in_specs=in_specs, out_specs=out_specs, check_vma=False)
```

time: 176 us -> 126 us (0.72)
  the two profiles are of different devices: /device:TPU:63 before, /device:TPU:31 now
where the time goes in v2:
time: 126 us
  Pallas kernels  122 us (97%)
  local copies, waits for them, and re-layouts  3.25 us (3%)
    pallas_call x1, Pallas kernels, shards(): pl.pallas_call(functools.partial(kernel, queue_len, nz), out_shape=(jax.S...  122 us
    unnamed x2, local copies, waits for them, and re-layouts  3.25 us

profile of v2, /device:TPU:31, one launch (start us, length us, event | category | flops | bytes accessed | tf_op | source)
XLA Modules:
  0.0 125.9 jit_solution(8134836006528920803)
XLA Ops:
  0.6 122.0 %shard_map.113 = (bf16[256,384]{1,0:T(8,128)(2,1)}, bf16[256,384]{1,0:T(8,128)(2,1)}) custom-call(f32[1000]{0:T(1024)} %sigma_hbm.1, s32[64]{0:T(128)} %tsteps_hbm.1, s32[64]{0:T(128)} %frames_hbm.1, f32[8,384]{1,0:T(8,128)} %constant.4.clone.pfreq_hbm, f32[1,128]{1,0:T(1,128)} %constant.5.clone.tfreq_hbm, bf16[256,384]{1,0:T(8,128)(2,1)} %states_hbm.1, ...), custom_call_target="tpu_custom_call" | custom-call | tf_op jit(solution)/shard_map/pallas_call | solution.py:723
  122.7 1.6 %copy.14 = bf16[256,384]{1,0:T(8,128)(2,1)} copy(bf16[256,384]{1,0:T(8,128)(2,1)} %get-tuple-element.4) | data formatting | bytes 393216
  124.3 1.6 %copy.15 = bf16[256,384]{1,0:T(8,128)(2,1)} copy(bf16[256,384]{1,0:T(8,128)(2,1)} %get-tuple-element.5) | data formatting | bytes 393216

commit v3 on v2

--- a/solution.py
+++ b/solution.py
@@ -16,8 +16,8 @@
 NX = 4
 NY = 8
 CORES = 2
-AG_PARTS = 4
-RS_PARTS = 4
+PARTS = 4
+LATER_PARTS = (2, 0, 3, 1)
 LANES = 128
 F32 = jnp.float32
 BF16 = jnp.bfloat16
@@ -44,7 +44,8 @@
     vel_ref,
     xg,
     h,
-    wg,
+    wkv,
+    wqr,
     wo,
     wm,
     acc,
@@ -60,6 +61,7 @@
     pos,
     sg,
     modg,
+    gate_ref,
     mean_b,
     rstd_b,
     sigma_ref,
@@ -139,10 +141,9 @@
     ]
     states_copy = pltpu.make_async_copy(states_hbm, xg.at[0, z], in_sem.at[5])
     wq_copies = [
-        pltpu.make_async_copy(
-            wq_hbm.at[c], wg.at[y, x, core, :, c * local_hh : (c + 1) * local_hh], in_sem.at[6 + c]
-        )
-        for c in range(3)
+        pltpu.make_async_copy(wq_hbm.at[0], wqr.at[y, x, core], in_sem.at[6]),
+        pltpu.make_async_copy(wq_hbm.at[1], wkv.at[y, x, core, :, 0:local_hh], in_sem.at[7]),
+        pltpu.make_async_copy(wq_hbm.at[2], wkv.at[y, x, core, :, local_hh : 2 * local_hh], in_sem.at[8]),
     ]
     states_copy.start()
     for copy in wq_copies + scalar_copies:
@@ -150,7 +151,7 @@
 
     barrier = pltpu.get_barrier_semaphore()
     partners = [at_z(d) for d in range(1, nz)]
-    partners += [at_x(1), at_x(-1), at_y(1), at_y(-1), sibling, after, before]
+    partners += [at_x(1), at_x(-1), at_x(2), at_y(1), at_y(-1), sibling, after, before]
     for partner in partners:
         pl.semaphore_signal(barrier, inc=1, device_id=partner, device_id_type=MESH)
 
@@ -200,7 +201,7 @@
         squares = jnp.sum(squares, axis=1, keepdims=True)
         lane = lax.broadcasted_iota(jnp.int32, (tokf, LANES), 1)
         both = jnp.where(lane == 0, sums, jnp.where(lane == 1, squares, 0.0))
-        sg[step, z] = both.T[0:8]
+        sg[step, z] = both.T[0:2]
 
     def sums_copy(step, d):
         return remote(sg.at[step, z], sg.at[step, z], st_send.at[step, d], st_recv.at[step, d], at_z(d))
@@ -222,10 +223,10 @@
         rstd_b[...] = jnp.broadcast_to(rstd, (LANES, tokf)).T
 
     last_hop = nz // 2 - 1
-    part_rows = tokf // AG_PARTS
+    part_rows = tokf // PARTS
 
     def ag_goes(direction, r, part):
-        return r < last_hop or part // (AG_PARTS // 2) == direction
+        return r < last_hop or part // (PARTS // 2) == direction
 
     def ag_remote(step, direction, r, part, k):
         ref = xg.at[step, k, pl.ds(part * part_rows, part_rows), :]
@@ -257,26 +258,33 @@
         for t in range(tiles):
             u = xg[step, k, :, lanes(t)].astype(F32) + row[:, lanes(t)]
             normed = (u - mean_b[...]) * rstd_b[...]
-            h[k, :, lanes(t)] = (normed * scale[:, lanes(t)] + shift[:, lanes(t)]).astype(BF16)
-
-    def project(k):
-        weights = wg[k].reshape(width, 3 * local_hh)
-        acc[...] += jnp.dot(h[k], weights, preferred_element_type=F32)
+            h[:, pl.ds(pl.multiple_of(k * width + t * LANES, LANES), LANES)] = (normed * scale[:, lanes(t)] + shift[:, lanes(t)]).astype(BF16)
+
+    def block_of_h(k):
+        return h[:, pl.ds(pl.multiple_of(k * width, LANES), width)]
+
+    def project_kv(k):
+        weights = wkv[k].reshape(width, 2 * local_hh)
+        acc[:, local_hh:] += jnp.dot(block_of_h(k), weights, preferred_element_type=F32)
+
+    def project_query(k):
+        weights = wqr[k].reshape(width, local_hh)
+        acc[:, :local_hh] += jnp.dot(block_of_h(k), weights, preferred_element_type=F32)
 
     near_x = (0, 3, 1, 2)
     near_y = (0, 1, 7, 2, 6, 3, 5, 4)
     far = NY // 2
 
-    def piece(c, dy, dx):
-        return wg.at[ring(y, dy, NY), ring(x, dx, NX), c]
-
-    def w_remote(index, ref, device):
-        return remote(ref, ref, w_send.at[index], w_recv.at[index], device)
-
-    def s_remote(c, dy, dx):
+    def piece(g, c, dy, dx):
+        return (wqr if g else wkv).at[ring(y, dy, NY), ring(x, dx, NX), c]
+
+    def w_remote(g, index, ref, device):
+        return remote(ref, ref, w_send.at[g, index], w_recv.at[g, index], device)
+
+    def s_remote(g, c, dy, dx):
         index = near_y.index(dy) * NX + near_x.index(dx)
-        ref = piece(c, dy, dx)
-        return remote(ref, ref, s_send.at[index], s_recv.at[index], sibling)
+        ref = piece(g, c, dy, dx)
+        return remote(ref, ref, s_send.at[g, index], s_recv.at[g, index], sibling)
 
     def both_x(dx):
         return at_x(1) if dx == 0 else at_x(-1)
@@ -293,174 +301,197 @@
     def c0_dy(r, direction):
         return (-r if direction == 0 else r) % NY
 
-    def c0_y_copy(r, direction, i):
-        return w_remote(c0_index(r, direction, i), piece(0, c0_dy(r, direction), near_x[i]), both_y(direction))
-
-    def c0_y_arrival(r, direction, i):
-        return w_remote(c0_index(r, direction, i), piece(0, c0_dy(r + 1, direction), near_x[i]), both_y(direction))
-
-    def c0_row(i):
+    def half_piece(ref, direction):
+        return ref.at[pl.ds(0, 32)] if direction == 0 else ref.at[pl.ds(32, 16)]
+
+    def c0_y_copy(g, r, direction, i):
+        return w_remote(g, c0_index(r, direction, i), piece(g, 0, c0_dy(r, direction), near_x[i]), both_y(direction))
+
+    def c0_y_arrival(g, r, direction, i):
+        return w_remote(g, c0_index(r, direction, i), piece(g, 0, c0_dy(r + 1, direction), near_x[i]), both_y(direction))
+
+    def c0_row(g, i):
         for direction in range(2):
-            c0_y_copy(0, direction, i).start()
-        s_remote(0, 0, near_x[i]).start()
-
-    def c0_x_copies():
+            c0_y_copy(g, 0, direction, i).start()
+        s_remote(g, 0, 0, near_x[i]).start()
+
+    def c0_x_copies(g):
         return [
-            w_remote(0, piece(0, 0, 0), at_x(1)),
-            w_remote(1, piece(0, 0, 0), at_x(-1)),
-            w_remote(2, piece(0, 0, 3), at_x(1)),
+            w_remote(g, 0, piece(g, 0, 0, 0), at_x(1)),
+            w_remote(g, 1, piece(g, 0, 0, 0), at_x(-1)),
+            w_remote(g, 2, piece(g, 0, 0, 0), at_x(2)),
         ]
 
-    def c0_start():
-        copies = c0_x_copies()
-        copies[0].start()
-        copies[1].start()
-        c0_row(0)
-
-    def c0_first_x():
-        w_remote(0, piece(0, 0, 3), at_x(1)).wait_recv()
-        c0_x_copies()[2].start()
-        c0_row(1)
-        w_remote(1, piece(0, 0, 1), at_x(-1)).wait_recv()
-        c0_row(2)
-
-    def c0_second_x():
-        w_remote(2, piece(0, 0, 2), at_x(1)).wait_recv()
-        c0_row(3)
-
-    def c0_y(r, i):
+    def c0_start(g):
+        for copy in c0_x_copies(g):
+            copy.start()
+        c0_row(g, 0)
+
+    def c0_first_x(g):
+        w_remote(g, 0, piece(g, 0, 0, 3), at_x(1)).wait_recv()
+        c0_row(g, 1)
+        w_remote(g, 1, piece(g, 0, 0, 1), at_x(-1)).wait_recv()
+        c0_row(g, 2)
+
+    def c0_second_x(g):
+        w_remote(g, 2, piece(g, 0, 0, 2), at_x(1)).wait_recv()
+        c0_row(g, 3)
+
+    def c0_y(g, r, i):
         def event():
             for direction in range(2):
                 if c0_goes(r, direction, i):
-                    c0_y_arrival(r, direction, i).wait_recv()
+                    c0_y_arrival(g, r, direction, i).wait_recv()
                     if r < far - 1 and c0_goes(r + 1, direction, i):
-                        c0_y_copy(r + 1, direction, i).start()
-                    s_remote(0, c0_dy(r + 1, direction), near_x[i]).start()
+                        c0_y_copy(g, r + 1, direction, i).start()
+                    s_remote(g, 0, c0_dy(r + 1, direction), near_x[i]).start()
 
         return event
 
-    def c1_y_part(r, direction, dy):
-        ref = piece(1, dy, 0)
-        if r == far - 1:
-            ref = ref.at[pl.ds(0, 32)] if direction == 0 else ref.at[pl.ds(32, 16)]
-        return ref
-
-    def c1_y_copy(r, direction):
-        return w_remote(2 * r + direction, c1_y_part(r, direction, c0_dy(r, direction)), both_y(direction))
-
-    def c1_y_arrival(r, direction):
-        return w_remote(2 * r + direction, c1_y_part(r, direction, c0_dy(r + 1, direction)), both_y(direction))
-
-    def c1_first(n, direction, dx):
-        return w_remote(8 + direction * NY + n, piece(1, near_y[n], dx), at_x(1 if direction == 0 else -1))
-
-    def c1_second(n, dx):
-        return w_remote(24 + n, piece(1, near_y[n], dx), at_x(1 if n % 2 == 0 else -1))
-
-    def c1_column(n):
+    def c1_y_part(g, r, direction, dy):
+        ref = piece(g, 1, dy, 0)
+        return half_piece(ref, direction) if r == far - 1 else ref
+
+    def c1_y_copy(g, r, direction):
+        return w_remote(g, 2 * r + direction, c1_y_part(g, r, direction, c0_dy(r, direction)), both_y(direction))
+
+    def c1_y_arrival(g, r, direction):
+        return w_remote(g, 2 * r + direction, c1_y_part(g, r, direction, c0_dy(r + 1, direction)), both_y(direction))
+
+    def c1_first(g, n, direction, dx):
+        return w_remote(g, 8 + direction * NY + n, piece(g, 1, near_y[n], dx), at_x(1 if direction == 0 else -1))
+
+    def c1_second(g, n, dx):
+        return w_remote(g, 24 + n, piece(g, 1, near_y[n], dx), at_x(1 if n % 2 == 0 else -1))
+
+    def c1_column(g, n):
         for direction in range(2):
-            c1_first(n, direction, 0).start()
-        s_remote(1, near_y[n], 0).start()
-
-    def c1_start():
+            c1_first(g, n, direction, 0).start()
+        s_remote(g, 1, near_y[n], 0).start()
+
+    def c1_start(g):
         for direction in range(2):
-            c1_y_copy(0, direction).start()
-        c1_column(0)
-
-    def c1_y(r):
+            c1_y_copy(g, 0, direction).start()
+        c1_column(g, 0)
+
+    def c1_y(g, r):
         def event():
             for direction in range(2):
-                c1_y_arrival(r, direction).wait_recv()
+                c1_y_arrival(g, r, direction).wait_recv()
                 if r < far - 1:
-                    c1_y_copy(r + 1, direction).start()
-            if r < far - 1:
-                c1_column(2 * r + 1)
-                c1_column(2 * r + 2)
-            else:
-                c1_column(NY - 1)
+                    c1_y_copy(g, r + 1, direction).start()
 
         return event
 
-    def c1_x(n):
+    def c1_send(g, n):
         def event():
-            c1_first(n, 0, 3).wait_recv()
+            c1_column(g, n)
+
+        return event
+
+    def c1_x(g, n):
+        def event():
+            c1_first(g, n, 0, 3).wait_recv()
             if n % 2 == 0:
-                c1_second(n, 3).start()
-            c1_first(n, 1, 1).wait_recv()
+                c1_second(g, n, 3).start()
+            c1_first(g, n, 1, 1).wait_recv()
             if n % 2 == 1:
-                c1_second(n, 1).start()
-            s_remote(1, near_y[n], 3).start()
-            s_remote(1, near_y[n], 1).start()
+                c1_second(g, n, 1).start()
+            s_remote(g, 1, near_y[n], 3).start()
+            s_remote(g, 1, near_y[n], 1).start()
 
         return event
 
-    def c1_xx(n):
+    def c1_xx(g, n):
         def event():
-            c1_second(n, 2).wait_recv()
-            s_remote(1, near_y[n], 2).start()
+            c1_second(g, n, 2).wait_recv()
+            s_remote(g, 1, near_y[n], 2).start()
 
         return event
 
-    c0_events = [[c0_first_x], [c0_y(0, 0)], [c0_second_x, c0_y(0, 1)], [c0_y(0, 2), c0_y(0, 3)]]
-    c0_events += [[c0_y(r, i)] for r in range(1, far) for i in range(NX)]
-    c1_events = [
-        [c1_y(0)],
-        [c1_x(0)],
-        [c1_y(1)],
-        [c1_x(1), c1_x(2)],
-        [c1_xx(0)],
-        [c1_y(2)],
-        [c1_x(3), c1_x(4)],
-        [c1_xx(1), c1_xx(2)],
-        [c1_y(3)],
-        [c1_x(5), c1_x(6)],
-        [c1_xx(3)],
-        [c1_xx(4)],
-        [c1_x(7)],
-        [c1_xx(5)],
-        [c1_xx(6)],
-        [c1_xx(7)],
-    ]
-
-    def weights_events(slot):
+    def c0_events(g):
+        return [
+            [functools.partial(c0_first_x, g)],
+            [c0_y(g, 0, 0)],
+            [functools.partial(c0_second_x, g)],
+            [c0_y(g, 0, 1)],
+            [c0_y(g, 0, 2)],
+            [c0_y(g, 1, 0)],
+            [c0_y(g, 0, 3)],
+            [c0_y(g, 1, 1)],
+            [c0_y(g, 1, 2)],
+            [c0_y(g, 2, 0)],
+            [c0_y(g, 1, 3)],
+            [c0_y(g, 2, 1)],
+            [c0_y(g, 2, 2)],
+            [c0_y(g, 3, 0)],
+            [c0_y(g, 2, 3)],
+            [c0_y(g, 3, 1)],
+            [c0_y(g, 3, 2)],
+            [c0_y(g, 3, 3)],
+        ]
+
+    def c1_events(g):
+        return [
+            [c1_y(g, 0)],
+            [c1_x(g, 0), c1_send(g, 1)],
+            [],
+            [c1_y(g, 1), c1_send(g, 2)],
+            [c1_x(g, 1), c1_send(g, 3)],
+            [c1_xx(g, 0), c1_x(g, 2), c1_send(g, 4)],
+            [],
+            [c1_y(g, 2)],
+            [c1_x(g, 3), c1_send(g, 5)],
+            [c1_xx(g, 1), c1_x(g, 4), c1_send(g, 6)],
+            [c1_xx(g, 2)],
+            [c1_y(g, 3)],
+            [c1_x(g, 5), c1_send(g, 7)],
+            [c1_xx(g, 3), c1_x(g, 6)],
+            [c1_xx(g, 4)],
+            [c1_x(g, 7)],
+            [c1_xx(g, 5), c1_xx(g, 6)],
+            [c1_xx(g, 7)],
+        ]
+
+    def weights_events(g, slot):
         @pl.when(core == 0)
         def _():
-            for event in c0_events[slot]:
+            for event in c0_events(g)[slot]:
                 event()
 
         @pl.when(core == 1)
         def _():
-            for event in c1_events[slot]:
+            for event in c1_events(g)[slot]:
                 event()
 
-    def from_sibling(n):
+    def from_sibling(g, n):
         for c in range(CORES):
 
             @pl.when(core != c)
             def _():
                 for dx in near_x:
-                    s_remote(c, near_y[n], dx).wait_recv()
-
-    def weights_drain():
+                    s_remote(g, c, near_y[n], dx).wait_recv()
+
+    def weights_drain(g):
         @pl.when(core == 0)
         def _():
-            for copy in c0_x_copies():
+            for copy in c0_x_copies(g):
                 copy.wait_send()
             for r in range(far):
                 for direction in range(2):
                     for i in range(NX):
                         if c0_goes(r, direction, i):
-                            c0_y_copy(r, direction, i).wait_send()
+                            c0_y_copy(g, r, direction, i).wait_send()
 
         @pl.when(core == 1)
         def _():
             for r in range(far):
                 for direction in range(2):
-                    c1_y_copy(r, direction).wait_send()
+                    c1_y_copy(g, r, direction).wait_send()
             for n in range(NY):
                 for direction in range(2):
-                    c1_first(n, direction, 0).wait_send()
-                c1_second(n, 3 if n % 2 == 0 else 1).wait_send()
+                    c1_first(g, n, direction, 0).wait_send()
+                c1_second(g, n, 3 if n % 2 == 0 else 1).wait_send()
 
         for c in range(CORES):
 
@@ -468,15 +499,23 @@
             def _():
                 for dy in near_y:
                     for dx in near_x:
-                        s_remote(c, dy, dx).wait_send()
-
-    rs_rows = tokf // RS_PARTS
+                        s_remote(g, c, dy, dx).wait_send()
+
+    first_order = [
+        "w0", "w1", "w2", "v0", "a00", "v1", "v2", "a01", "w3", "a02", "w4", "a03", "w5", "w6", "a10", "v3",
+        "v4", "a11", "w7", "v5", "v6", "a12", "w8", "a13", "w9", "v7", "w10", "v8", "a20", "a21", "w11", "v9",
+        "a22", "w12", "v10", "a23", "w13", "v11", "m", "w14", "v12", "a30", "w15", "v13", "a31", "w16", "v14", "a32",
+        "w17", "v15", "a33", "v16", "m", "k", "s", "v17", "q",
+    ]
+    later_order = ["a%d%d" % (r, part) for r in range(nz // 2) for part in LATER_PARTS]
+
+    rs_rows = tokf // PARTS
 
     def rows_of(part):
         return pl.ds(part * rs_rows, rs_rows)
 
     def rs_goes(direction, s, part):
-        return s > 0 or part // (RS_PARTS // 2) == direction
+        return s > 0 or part // (PARTS // 2) == direction
 
     def rs_remote(step, direction, s, part):
         rows = rows_of(part)
@@ -509,9 +548,10 @@
 
     for d in range(1, nz):
         sums_copy(0, d).start()
-    pl.when(core == 0)(c0_start)
-    pl.when(core == 1)(c1_start)
-    for part in range(AG_PARTS):
+    for g in range(2):
+        pl.when(core == 0)(functools.partial(c0_start, g))
+        pl.when(core == 1)(functools.partial(c1_start, g))
+    for part in range(PARTS):
         for direction in range(2):
             ag_copy(0, direction, 0, part).start()
 
@@ -523,10 +563,13 @@
     low = (emb - high - middle).astype(BF16).astype(F32)
     index = lax.broadcasted_iota(jnp.int32, (16, TEMB), 0)
     parts = jnp.where(index == 0, high, jnp.where(index == 1, middle, jnp.where(index == 2, low, 0.0)))
-    modg[z] = jnp.zeros((8, width), F32)
     for c in range(3):
         modul = jnp.dot(parts.astype(BF16), wm[c], preferred_element_type=F32)
-        modg[z, c : c + 1, :] = jnp.sum(modul, axis=0, keepdims=True)
+        modul = jnp.sum(modul, axis=0, keepdims=True)
+        if c < 2:
+            modg[z, c : c + 1, :] = modul
+        else:
+            gate_ref[...] = modul
 
     def mod_copy(d):
         return remote(modg.at[z], modg.at[z], mod_send.at[d], mod_recv.at[d], at_z(d))
@@ -539,65 +582,84 @@
         mod_copy(d).start()
 
     acc[...] = jnp.zeros_like(acc)
+    def begin(step):
+        @pl.when(last_slot)
+        def _():
+            noise_copy.wait()
+            xg[step, z] = fresh[(step - 1) * tokf : step * tokf]
+
+        for part in LATER_PARTS:
+
+            @pl.when(jnp.logical_not(last_slot))
+            def _():
+                sh_arrival(step - 1, part).wait_recv()
+
+            for direction in range(2):
+                ag_copy(step, direction, 0, part).start()
+        own_sums(step)
+        for d in range(1, nz):
+            sums_copy(step, d).start()
+
     for step in range(STEPS):
         if step > 0:
-            @pl.when(jnp.logical_not(last_slot))
-            def _():
-                for part in range(RS_PARTS):
-                    sh_arrival(0, part).wait_recv()
-
-            @pl.when(last_slot)
-            def _():
-                noise_copy.wait()
-                xg[1, z] = fresh[0:tokf]
-
-            own_sums(step)
-            for d in range(1, nz):
-                sums_copy(step, d).start()
-            for part in range(AG_PARTS):
-                for direction in range(2):
-                    ag_copy(step, direction, 0, part).start()
             acc[...] = jnp.zeros_like(acc)
+        def kv_arrival(c):
+            return remote(kv.at[step, c], prev.at[step, c], kv_send.at[step, c], kv_recv.at[step, c], after)
+
+        def send_kv():
+            for c in range(2):
+                kv[step, c] = acc[:, (c + 1) * local_hh : (c + 2) * local_hh].astype(BF16)
+                kv_arrival(c).start()
+
         ready = [z]
         formed = False
-        for r in range(nz // 2):
-            for part in range(AG_PARTS):
+        for i, item in enumerate(first_order if step == 0 else later_order):
+            kind, number = item[0], int(item[1:] or 0)
+            if kind in "wv":
+                weights_events("wv".index(kind), number)
+            elif kind in "kq":
+                for n in range(NY):
+                    from_sibling("kq".index(kind), n)
+                if kind == "k":
+                    acc[:, local_hh:] = jnp.dot(
+                        h[...], wkv[...].reshape(full, 2 * local_hh), preferred_element_type=F32
+                    )
+                else:
+                    acc[:, :local_hh] = jnp.dot(
+                        h[...], wqr[...].reshape(full, local_hh), preferred_element_type=F32
+                    )
+            elif kind == "m":
+                if not formed:
+                    formed = True
+                    for d in range(1, nz):
+                        mod_arrival(d).wait_recv()
+                    finish_sums(step)
+                for k in ready:
+                    modulate(step, k)
+                ready = []
+            elif kind == "s":
+                send_kv()
+            else:
+                r, part = number // 10, number % 10
                 ag_forward(step, r, part)
-                if step == 0 and r < last_hop:
-                    weights_events(r * AG_PARTS + part)
-                if (r, part) == ((nz // 2 - 2, 0) if step == 0 else (0, 0)):
+                if step > 0 and i == PARTS + 1:
                     formed = True
-                    if step == 0:
-                        for d in range(1, nz):
-                            mod_arrival(d).wait_recv()
                     finish_sums(step)
-                if ready and formed and (step == 0 or part % 2 == 1):
+                if step > 0 and ready and formed:
                     k = ready.pop(0)
                     modulate(step, k)
-                    if step > 0:
-                        project(k)
-            ready += [ring(z, -r - 1, nz), ring(z, r + 1, nz)] if r < last_hop else [ring(z, nz // 2, nz)]
-        for k in ready:
-            modulate(step, k)
-            if step > 0:
-                project(k)
-        if step == 0:
-            for part in range(AG_PARTS):
-                weights_events(last_hop * AG_PARTS + part)
-                for n in ((0, 1), (2,), (3,), (4,))[part]:
-                    from_sibling(n)
-                    project(ring(y, near_y[n], NY))
-            for n in range(5, NY):
-                from_sibling(n)
-                project(ring(y, near_y[n], NY))
-
-        for c in range(2):
-            kv[step, c] = acc[:, (c + 1) * local_hh : (c + 2) * local_hh].astype(BF16)
-            remote(kv.at[step, c], prev.at[step, c], kv_send.at[step, c], kv_recv.at[step, c], after).start()
+                    project_kv(k)
+                    project_query(k)
+                if part == (PARTS - 1 if step == 0 else LATER_PARTS[-1]):
+                    ready += [ring(z, -r - 1, nz), ring(z, r + 1, nz)] if r < last_hop else [ring(z, nz // 2, nz)]
+        if step > 0:
+            for k in ready:
+                modulate(step, k)
+                project_kv(k)
+            send_kv()
+            for k in ready:
+                project_query(k)
         query[...] = acc[:, 0:local_hh].astype(BF16)
-
-        def kv_arrival(c):
-            return remote(kv.at[step, c], prev.at[step, c], kv_send.at[step, c], kv_recv.at[step, c], after)
 
         def scores(keys):
             s = lax.dot_general(
@@ -634,31 +696,34 @@
                 rs_out[step, direction, s, side * half : (side + 1) * half, :] = rs_term(
                     direction, s, side * half, half
                 ).astype(BF16)
-                for part in range(RS_PARTS):
-                    if part // (RS_PARTS // 2) == side:
+                for part in range(PARTS):
+                    if part // (PARTS // 2) == side:
                         rs_remote(step, direction, s, part).start()
         for s in range(1, nz // 2):
             for direction in range(2):
                 if s == 1:
                     rows = slice(direction * half, (direction + 1) * half)
-                    term[direction, rows, :] = rs_term(direction, s, direction * half, half)
+                    term[s, direction, rows, :] = rs_term(direction, s, direction * half, half)
                 else:
-                    term[direction] = rs_term(direction, s, 0, tokf)
-            for i in range(RS_PARTS):
+                    term[s, direction] = rs_term(direction, s, 0, tokf)
+        term[0, 0] = rs_term(0, nz // 2, 0, tokf)
+        for s in range(1, nz // 2):
+            for i in range(PARTS):
                 for direction in range(2):
-                    part = (i + RS_PARTS // 2 * (1 - direction)) % RS_PARTS
+                    part = (i + PARTS // 2 * (1 - direction)) % PARTS
                     if rs_goes(direction, s - 1, part):
                         rows = rows_of(part)
                         rs_remote(step, direction, s - 1, part).wait_recv()
                         rs_out[step, direction, s, rows, :] = (
-                            rs_in[step, direction, s - 1, rows, :].astype(F32) + term[direction, rows, :]
+                            rs_in[step, direction, s - 1, rows, :].astype(F32) + term[s, direction, rows, :]
                         ).astype(BF16)
                         rs_remote(step, direction, s, part).start()
-        term[0] = rs_term(0, nz // 2, 0, tokf)
-        gate = modg[z][2:3]
-        for part in (2, 0, 3, 1):
+        if step < STEPS - 1:
+            pl.when(core == 0)(functools.partial(begin, step + 1))
+        gate = gate_ref[...]
+        for part in LATER_PARTS:
             rows = rows_of(part)
-            summed = term[0, rows, :]
+            summed = term[0, 0, rows, :]
             for direction in range(2):
                 rs_remote(step, direction, nz // 2 - 1, part).wait_recv()
                 summed = summed + rs_in[step, direction, nz // 2 - 1, rows, :].astype(F32)
@@ -671,27 +736,31 @@
             def _():
                 sh_copy(step, part).start()
 
+        if step < STEPS - 1:
+            pl.when(core == 1)(functools.partial(begin, step + 1))
+
     @pl.when(last_slot)
     def _():
         new_ref[...] = fresh[tokf : 2 * tokf]
 
     @pl.when(jnp.logical_not(last_slot))
     def _():
-        for part in range(RS_PARTS):
+        for part in range(PARTS):
             sh_arrival(1, part).wait_recv()
 
-    weights_drain()
+    for g in range(2):
+        weights_drain(g)
     for d in range(1, nz):
         mod_copy(d).wait_send()
     for step in range(STEPS):
         for d in range(1, nz):
             sums_copy(step, d).wait_send()
         for direction in range(2):
-            for part in range(AG_PARTS):
+            for part in range(PARTS):
                 for r in range(nz // 2):
                     if ag_goes(direction, r, part):
                         ag_copy(step, direction, r, part).wait_send()
-            for part in range(RS_PARTS):
+            for part in range(PARTS):
                 for hop in range(nz // 2):
                     if rs_goes(direction, hop, part):
                         rs_remote(step, direction, hop, part).wait_send()
@@ -701,7 +770,7 @@
     @pl.when(q > 0)
     def _():
         for step in range(STEPS):
-            for part in range(RS_PARTS):
+            for part in range(PARTS):
                 sh_copy(step, part).wait_send()
 
 
@@ -730,8 +799,9 @@
             out_specs=(vmem, vmem),
             scratch_shapes=[
                 pltpu.VMEM((STEPS, nz, tokf, width), BF16),
-                pltpu.VMEM((nz, tokf, width), BF16),
-                pltpu.VMEM((NY, NX, CORES, rows, 3 * local_hh), BF16),
+                pltpu.VMEM((tokf, nz * width), BF16),
+                pltpu.VMEM((NY, NX, CORES, rows, 2 * local_hh), BF16),
+                pltpu.VMEM((NY, NX, CORES, rows, local_hh), BF16),
                 pltpu.VMEM((nz, local_hh, width), BF16),
                 pltpu.VMEM((3, TEMB, width), BF16),
                 pltpu.VMEM((tokf, 3 * local_hh), F32),
@@ -742,11 +812,12 @@
                 pltpu.VMEM((STEPS, 2, hops, tokf, width), BF16),
                 pltpu.VMEM((STEPS, 2, hops, tokf, width), BF16),
                 pltpu.VMEM((STEPS, tokf, width), BF16),
-                pltpu.VMEM((2, tokf, width), F32),
+                pltpu.VMEM((hops, 2, tokf, width), F32),
                 pltpu.VMEM((STEPS * tokf, width), BF16),
                 pltpu.VMEM((STEPS, nz, width), F32),
-                pltpu.VMEM((STEPS, nz, 8, tokf), F32),
-                pltpu.VMEM((nz, 8, width), F32),
+                pltpu.VMEM((STEPS, nz, 2, tokf), F32),
+                pltpu.VMEM((nz, 2, width), F32),
+                pltpu.VMEM((1, width), F32),
                 pltpu.VMEM((tokf, LANES), F32),
                 pltpu.VMEM((tokf, LANES), F32),
                 pltpu.SMEM(sigma_table.shape, F32),
@@ -758,22 +829,22 @@
                 dma((nz,)),
                 dma,
                 dma,
-                dma((STEPS, 2, hops, AG_PARTS)),
-                dma((STEPS, 2, hops, AG_PARTS)),
-                dma((35,)),
-                dma((35,)),
-                dma((NY * NX,)),
-                dma((NY * NX,)),
+                dma((STEPS, 2, hops, PARTS)),
+                dma((STEPS, 2, hops, PARTS)),
+                dma((2, 35)),
+                dma((2, 35)),
+                dma((2, NY * NX)),
+                dma((2, NY * NX)),
                 dma((STEPS, nz)),
                 dma((STEPS, nz)),
                 dma((nz,)),
                 dma((nz,)),
                 dma((STEPS, 2)),
                 dma((STEPS, 2)),
-                dma((STEPS, 2, hops, RS_PARTS)),
-                dma((STEPS, 2, hops, RS_PARTS)),
-                dma((STEPS, RS_PARTS)),
-                dma((STEPS, RS_PARTS)),
+                dma((STEPS, 2, hops, PARTS)),
+                dma((STEPS, 2, hops, PARTS)),
+                dma((STEPS, PARTS)),
+                dma((STEPS, PARTS)),
             ],
             compiler_params=pltpu.CompilerParams(
                 collective_id=0, has_side_effects=True, vmem_limit_bytes=60 * 1024 * 1024

time: 126 us -> 121 us (0.960)
  Pallas kernels: 122 us -> 117 us
    pallas_call x1, Pallas kernels: 122 us -> 117 us  [shards(): pl.pallas_call(functools.partial(kernel, queue_len, nz), out_shape=(jax.S...]
where the time goes in v3:
time: 121 us
  Pallas kernels  117 us (97%)
  local copies, waits for them, and re-layouts  3.25 us (3%)
    pallas_call x1, Pallas kernels, shards(): pl.pallas_call(functools.partial(kernel, queue_len, nz), out_shape=(jax.S...  117 us
    unnamed x2, local copies, waits for them, and re-layouts  3.25 us

profile of v3, /device:TPU:31, one launch (start us, length us, event | category | flops | bytes accessed | tf_op | source)
XLA Modules:
  0.0 120.9 jit_solution(2455333349068135681)
XLA Ops:
  0.6 117.1 %shard_map.113 = (bf16[256,384]{1,0:T(8,128)(2,1)}, bf16[256,384]{1,0:T(8,128)(2,1)}) custom-call(f32[1000]{0:T(1024)} %sigma_hbm.1, s32[64]{0:T(128)} %tsteps_hbm.1, s32[64]{0:T(128)} %frames_hbm.1, f32[8,384]{1,0:T(8,128)} %constant.4.clone.pfreq_hbm, f32[1,128]{1,0:T(1,128)} %constant.5.clone.tfreq_hbm, bf16[256,384]{1,0:T(8,128)(2,1)} %states_hbm.1, ...), custom_call_target="tpu_custom_call" | custom-call | tf_op jit(solution)/shard_map/pallas_call | solution.py:792
  117.7 1.6 %copy.14 = bf16[256,384]{1,0:T(8,128)(2,1)} copy(bf16[256,384]{1,0:T(8,128)(2,1)} %get-tuple-element.4) | data formatting | bytes 393216
  119.3 1.6 %copy.15 = bf16[256,384]{1,0:T(8,128)(2,1)} copy(bf16[256,384]{1,0:T(8,128)(2,1)} %get-tuple-element.5) | data formatting | bytes 393216

commit v4 on v3

--- a/solution.py
+++ b/solution.py
@@ -16,8 +16,8 @@
 NX = 4
 NY = 8
 CORES = 2
-PARTS = 4
-LATER_PARTS = (2, 0, 3, 1)
+PARTS = 8
+LATER_PARTS = tuple(i // 2 + (PARTS // 2 if i % 2 == 0 else 0) for i in range(PARTS))
 LANES = 128
 F32 = jnp.float32
 BF16 = jnp.bfloat16
@@ -267,6 +267,11 @@
         weights = wkv[k].reshape(width, 2 * local_hh)
         acc[:, local_hh:] += jnp.dot(block_of_h(k), weights, preferred_element_type=F32)
 
+    def project_last(k, c):
+        weights = wkv[k, :, :, :, c * local_hh : (c + 1) * local_hh].reshape(width, local_hh)
+        total = acc[:, (c + 1) * local_hh : (c + 2) * local_hh]
+        return (total + jnp.dot(block_of_h(k), weights, preferred_element_type=F32)).astype(BF16)
+
     def project_query(k):
         weights = wqr[k].reshape(width, local_hh)
         acc[:, :local_hh] += jnp.dot(block_of_h(k), weights, preferred_element_type=F32)
@@ -503,9 +508,10 @@
 
     first_order = [
         "w0", "w1", "w2", "v0", "a00", "v1", "v2", "a01", "w3", "a02", "w4", "a03", "w5", "w6", "a10", "v3",
-        "v4", "a11", "w7", "v5", "v6", "a12", "w8", "a13", "w9", "v7", "w10", "v8", "a20", "a21", "w11", "v9",
-        "a22", "w12", "v10", "a23", "w13", "v11", "m", "w14", "v12", "a30", "w15", "v13", "a31", "w16", "v14", "a32",
-        "w17", "v15", "a33", "v16", "m", "k", "s", "v17", "q",
+        "v4", "a11", "w7", "v5", "v6", "a12", "w8", "a13", "m", "w9", "v7", "w10", "v8", "a20", "m", "a21",
+        "w11", "v9", "a22", "w12", "v10", "a23", "w13", "v11", "w14", "v12", "a30", "m", "a31", "w15", "v13", "a32",
+        "a33", "m", "k0", "k1", "w16", "v14", "k2", "k3", "k4", "w17", "v15", "k5", "k6", "s", "v16", "v17",
+        "q",
     ]
     later_order = ["a%d%d" % (r, part) for r in range(nz // 2) for part in LATER_PARTS]
 
@@ -582,6 +588,7 @@
         mod_copy(d).start()
 
     acc[...] = jnp.zeros_like(acc)
+
     def begin(step):
         @pl.when(last_slot)
         def _():
@@ -603,12 +610,13 @@
     for step in range(STEPS):
         if step > 0:
             acc[...] = jnp.zeros_like(acc)
+
         def kv_arrival(c):
             return remote(kv.at[step, c], prev.at[step, c], kv_send.at[step, c], kv_recv.at[step, c], after)
 
-        def send_kv():
+        def send_kv(k):
             for c in range(2):
-                kv[step, c] = acc[:, (c + 1) * local_hh : (c + 2) * local_hh].astype(BF16)
+                kv[step, c] = project_last(k, c)
                 kv_arrival(c).start()
 
         ready = [z]
@@ -617,17 +625,13 @@
             kind, number = item[0], int(item[1:] or 0)
             if kind in "wv":
                 weights_events("wv".index(kind), number)
-            elif kind in "kq":
+            elif kind == "k":
+                from_sibling(0, number)
+                project_kv(ring(y, near_y[number], NY))
+            elif kind == "q":
                 for n in range(NY):
-                    from_sibling("kq".index(kind), n)
-                if kind == "k":
-                    acc[:, local_hh:] = jnp.dot(
-                        h[...], wkv[...].reshape(full, 2 * local_hh), preferred_element_type=F32
-                    )
-                else:
-                    acc[:, :local_hh] = jnp.dot(
-                        h[...], wqr[...].reshape(full, local_hh), preferred_element_type=F32
-                    )
+                    from_sibling(1, n)
+                acc[:, :local_hh] = jnp.dot(h[...], wqr[...].reshape(full, local_hh), preferred_element_type=F32)
             elif kind == "m":
                 if not formed:
                     formed = True
@@ -638,10 +642,12 @@
                     modulate(step, k)
                 ready = []
             elif kind == "s":
-                send_kv()
+                from_sibling(0, NY - 1)
+                send_kv(ring(y, near_y[-1], NY))
             else:
                 r, part = number // 10, number % 10
-                ag_forward(step, r, part)
+                for p in range(part * PARTS // 4, (part + 1) * PARTS // 4) if step == 0 else (part,):
+                    ag_forward(step, r, p)
                 if step > 0 and i == PARTS + 1:
                     formed = True
                     finish_sums(step)
@@ -650,13 +656,14 @@
                     modulate(step, k)
                     project_kv(k)
                     project_query(k)
-                if part == (PARTS - 1 if step == 0 else LATER_PARTS[-1]):
+                if part == (3 if step == 0 else LATER_PARTS[-1]):
                     ready += [ring(z, -r - 1, nz), ring(z, r + 1, nz)] if r < last_hop else [ring(z, nz // 2, nz)]
         if step > 0:
             for k in ready:
                 modulate(step, k)
+            for k in ready[:-1]:
                 project_kv(k)
-            send_kv()
+            send_kv(ready[-1])
             for k in ready:
                 project_query(k)
         query[...] = acc[:, 0:local_hh].astype(BF16)
@@ -739,15 +746,6 @@
         if step < STEPS - 1:
             pl.when(core == 1)(functools.partial(begin, step + 1))
 
-    @pl.when(last_slot)
-    def _():
-        new_ref[...] = fresh[tokf : 2 * tokf]
-
-    @pl.when(jnp.logical_not(last_slot))
-    def _():
-        for part in range(PARTS):
-            sh_arrival(1, part).wait_recv()
-
     for g in range(2):
         weights_drain(g)
     for d in range(1, nz):
@@ -766,6 +764,15 @@
                         rs_remote(step, direction, hop, part).wait_send()
         for c in range(2):
             remote(kv.at[step, c], prev.at[step, c], kv_send.at[step, c], kv_recv.at[step, c], after).wait_send()
+
+    @pl.when(last_slot)
+    def _():
+        new_ref[...] = fresh[tokf : 2 * tokf]
+
+    @pl.when(jnp.logical_not(last_slot))
+    def _():
+        for part in range(PARTS):
+            sh_arrival(1, part).wait_recv()
 
     @pl.when(q > 0)
     def _():

time: 121 us -> 121 us (level)
  no operation moved by 1% of the time
where the time goes in v4:
time: 121 us; the launch traced here: 120 us
  Pallas kernels  117 us (97%)
  local copies, waits for them, and re-layouts  3.25 us (3%)
    pallas_call x1, Pallas kernels, shards(): pl.pallas_call(functools.partial(kernel, queue_len, nz), out_shape=(jax.S...  117 us
    unnamed x2, local copies, waits for them, and re-layouts  3.25 us

profile of v4, /device:TPU:31, one launch (start us, length us, event | category | flops | bytes accessed | tf_op | source)
XLA Modules:
  0.0 120.5 jit_solution(616229483925116687)
XLA Ops:
  0.6 116.6 %shard_map.113 = (bf16[256,384]{1,0:T(8,128)(2,1)}, bf16[256,384]{1,0:T(8,128)(2,1)}) custom-call(f32[1000]{0:T(1024)} %sigma_hbm.1, s32[64]{0:T(128)} %tsteps_hbm.1, s32[64]{0:T(128)} %frames_hbm.1, f32[8,384]{1,0:T(8,128)} %constant.4.clone.pfreq_hbm, f32[1,128]{1,0:T(1,128)} %constant.5.clone.tfreq_hbm, bf16[256,384]{1,0:T(8,128)(2,1)} %states_hbm.1, ...), custom_call_target="tpu_custom_call" | custom-call | tf_op jit(solution)/shard_map/pallas_call | solution.py:799
  117.2 1.6 %copy.14 = bf16[256,384]{1,0:T(8,128)(2,1)} copy(bf16[256,384]{1,0:T(8,128)(2,1)} %get-tuple-element.4) | data formatting | bytes 393216
  118.8 1.6 %copy.15 = bf16[256,384]{1,0:T(8,128)(2,1)} copy(bf16[256,384]{1,0:T(8,128)(2,1)} %get-tuple-element.5) | data formatting | bytes 393216
